TPU v7x, 32 devices: a whole 2x2x4 slice. The times are simulated.
32 devices in a mesh: dom: 16 (over z, x, core), frame: 2 (over y).
Axes of the slice: x: 2, y: 2, z: 4, core: 2. Of those that a mesh axis runs over, the one named last changes fastest.
Arguments:
- features: bfloat16 [2048, 512], P('dom'), may hold values from -6 to 6
- positions: bfloat16 [3, 2048], P(None, 'dom'), may hold values from 0 to 4
- neighbours: int32 [2048, 128], P('dom'), may hold values from 0 to 255, as said below
- counts: int32 [2048], P('dom'), may hold values from 1 to 128, as said below
- send_rows: int32 [16, 2, 64], P('dom'), may hold values from 0 to 127
- frames: float32 [2, 3, 3], P('frame')
- w_edge: float32 [9, 512], replicated, may hold values from -2 to 2
- b_edge: float32 [512], replicated, may hold values from -4 to 4
- w_message: bfloat16 [512, 512], replicated, may hold values from -0.25 to 0.25
- w_update: bfloat16 [512, 512], replicated, may hold values from -0.25 to 0.25
- w_readout: bfloat16 [512, 512], replicated, may hold values from -0.25 to 0.25
- w_heads: bfloat16 [512, 4], replicated, may hold values from -0.25 to 0.25
Outputs:
- predictions: float32 [4, 2048], P(None, 'dom')
Inputs may be any that keep to these rules, and one draw needn't show every extreme that they name: `counts`: each domain has its own largest count, one of 32, 64, 96 or 128, reached by one of its atoms; some domain reaches 128. `neighbours`: order a domain's table as the 64 rows from the domain below, its own 128 atoms, then the 64 rows from the domain above; every slot of an atom in aligned block b of 16 atoms of its domain names a row at positions (b * 128) // max(7, 1) to that plus 128 - 1 of this order.
All inputs are finite; a program needn't handle non-finite values.
Results may differ from a plain program's by a relative error of at most 0.0049.
Values may be sent and summed in bfloat16 or wider, within the bound.
A program may use at most 64 MiB of HBM per device.

v0:
```python
import jax
import jax.numpy as jnp
from jax import lax
from jax.sharding import PartitionSpec as P

WINDOW = 128


message_scale = 0.0884
radial_step = 1.25
block_atoms = 16


def padded(cells, sides, width):
    for axis, dim in sides:
        count = lax.axis_size(axis)
        head = lax.slice_in_dim(cells, 0, width, axis=dim)
        tail = lax.slice_in_dim(cells, cells.shape[dim] - width, cells.shape[dim], axis=dim)
        cells = jnp.concatenate(
            [
                lax.ppermute(tail, axis, [(i, (i + 1) % count) for i in range(count)]),
                cells,
                lax.ppermute(head, axis, [((i + 1) % count, i) for i in range(count)]),
            ],
            axis=dim,
        )
    return cells


def edge_messages(rows_feat, rows_pos, centre_pos, live_mask, rotation, w_edge, b_edge):
    relative = rows_pos - centre_pos[:, None, :]
    frame_vec = jnp.einsum("bkc,ac->bka", relative, rotation, precision=lax.Precision.HIGHEST)
    distance = jnp.sqrt(jnp.sum(relative * relative, axis=-1) + 0.25)
    centres = jnp.arange(w_edge.shape[0] - 3, dtype=jnp.float32) * radial_step
    radial = jnp.exp(-((distance[..., None] - centres) ** 2))
    edge_in = jnp.concatenate([radial, frame_vec], axis=-1)
    preact = jnp.einsum("bki,iw->bkw", edge_in, w_edge, precision=lax.Precision.HIGHEST) + b_edge
    edge_gate = jax.nn.silu(preact) * live_mask[..., None]
    return jnp.sum(edge_gate * rows_feat, axis=1) * message_scale


def fetch_rows(local_rows, window_feat, window_pos):
    picker = (local_rows[..., None] == lax.broadcasted_iota(jnp.int32, (1, 1, WINDOW), 2)).astype(
        jnp.bfloat16
    )
    flat_pick = picker.reshape(-1, WINDOW)
    got_feat = jnp.dot(flat_pick, window_feat, preferred_element_type=jnp.float32)
    got_pos = jnp.dot(flat_pick, window_pos, preferred_element_type=jnp.float32)
    shape_rows = local_rows.shape
    return (
        got_feat.reshape(shape_rows + (window_feat.shape[1],)),
        got_pos.reshape(shape_rows + (3,)),
    )


def local(
    features,
    positions,
    neighbours,
    counts,
    send_rows,
    frames,
    w_edge,
    b_edge,
    w_message,
    w_update,
    w_readout,
    w_heads,
):
    local_atoms = features.shape[0]
    feature_width = features.shape[1]
    slot_total = neighbours.shape[1]
    frame_count = lax.axis_size("frame")
    cap_rows = send_rows.shape[2]
    rows_pos = positions.T
    chosen = send_rows[0]
    chosen = chosen.reshape(-1)
    padded_feat, padded_pos = (
        padded(features[chosen], (("dom", 0),), cap_rows),
        padded(rows_pos[chosen], (("dom", 0),), cap_rows),
    )
    ghost_feat = jnp.concatenate([padded_feat[:cap_rows], padded_feat[-cap_rows:]], axis=0)
    ghost_pos = jnp.concatenate([padded_pos[:cap_rows], padded_pos[-cap_rows:]], axis=0)
    ordered_feat = jnp.concatenate([ghost_feat[:cap_rows], features, ghost_feat[cap_rows:]], axis=0)
    ordered_pos = jnp.concatenate([ghost_pos[:cap_rows], rows_pos, ghost_pos[cap_rows:]], axis=0)
    table_rows = ordered_feat.shape[0]
    block_total = local_atoms // block_atoms
    span_rows = table_rows - WINDOW
    denom = max(block_total - 1, 1)
    placed = jnp.where(
        neighbours < local_atoms,
        neighbours + cap_rows,
        jnp.where(neighbours < local_atoms + cap_rows, neighbours - local_atoms, neighbours),
    )
    block_ids = jnp.arange(block_total, dtype=jnp.int32)
    block_starts = block_ids * span_rows // denom
    rotation = frames[0]
    coords = rows_pos.astype(jnp.float32)
    block_inputs = (
        placed.reshape(-1, block_atoms, slot_total),
        counts.reshape(-1, block_atoms),
        coords.reshape(-1, block_atoms, 3),
        block_starts,
    )

    def one_block(block_in):
        block_idx, block_count, block_centre, block_start = block_in
        window_feat = lax.dynamic_slice_in_dim(ordered_feat, block_start, WINDOW, 0)
        window_pos = lax.dynamic_slice_in_dim(ordered_pos, block_start, WINDOW, 0)
        local_rows = block_idx - block_start
        slot_place = lax.broadcasted_iota(jnp.int32, block_idx.shape, 1)
        live_mask = (slot_place < block_count[:, None]).astype(jnp.float32)
        got_feat, got_pos = fetch_rows(local_rows, window_feat, window_pos)
        return edge_messages(got_feat, got_pos, block_centre, live_mask, rotation, w_edge, b_edge)

    message = (
        lax.map(one_block, block_inputs).reshape(local_atoms, feature_width).astype(jnp.bfloat16)
    )
    hidden = jax.nn.silu(jnp.dot(message, w_message, preferred_element_type=jnp.float32)).astype(
        jnp.bfloat16
    )
    updated = (
        features.astype(jnp.float32) + jnp.dot(hidden, w_update, preferred_element_type=jnp.float32)
    ).astype(jnp.bfloat16)
    readout = jax.nn.silu(jnp.dot(updated, w_readout, preferred_element_type=jnp.float32)).astype(
        jnp.bfloat16
    )
    heads = jnp.dot(readout, w_heads, preferred_element_type=jnp.float32)
    force_can = jnp.einsum("na,ac->cn", heads[:, :3], rotation, precision=lax.Precision.HIGHEST)
    frame_term = jnp.concatenate([force_can, heads[:, 3][None, :]], axis=0)
    return lax.psum(frame_term, "frame") / frame_count


def solution(mesh):
    placed = (
        P("dom", None),
        P(None, "dom"),
        P("dom", None),
        P("dom"),
        P("dom", None, None),
        P("frame", None, None),
        P(),
        P(),
        P(),
        P(),
        P(),
        P(),
    )
    return jax.shard_map(
        local, mesh=mesh, in_specs=placed, out_specs=P(None, "dom"), check_vma=False
    )
```

profile of v0, /device:TPU:0, one launch (start us, length us, event | category | flops | bytes accessed | tf_op | source)
XLA Modules:
  0.0 127.4 jit_solution(10572547211522466069)
XLA Ops:
  0.0 0.9 copy.18
  0.9 0.8 reshape_squeeze.3
  1.6 0.7 gather_fusion
  2.9 5.0 %collective-permute-start.1 = (bf16[64,3]{1,0:T(8,128)(2,1)S(1)}, bf16[64,3]{1,0:T(8,128)(2,1)S(1)}, u32[]{:S(2)}, u32[]{:S(2)}) collective-permute-start(bf16[64,3]{1,0:T(8,128)(2,1)S(1)} %get-tuple-element.112), channel_id=1, source_target_pairs={{2,0},{4,2},{6,4},{8,6},{10,8},{12,10},{14,12},{16,14},{18,16},{20... | collective-permute-start | bytes 1160 | tf_op jit(solution)/shard_map/ppermute | solution.py:23
  7.9 1.8 %gather_fusion.1 = bf16[128,512]{1,0:T(8,128)(2,1)S(1)} fusion(bf16[128,512]{1,0:T(8,128)(2,1)} %param.14, s32[1024]{0:T(1024)S(1)} %pad_clamp_fusion), kind=kCustom, calls=%fused_computation.1 | custom fusion | bytes 262656 | tf_op jit(solution)/shard_map/gather | solution.py:79
  9.8 4.4 %collective-permute-start.3 = (bf16[64,512]{1,0:T(8,128)(2,1)S(1)}, bf16[64,512]{1,0:T(8,128)(2,1)S(1)}, u32[]{:S(2)}, u32[]{:S(2)}) collective-permute-start(bf16[64,512]{1,0:T(8,128)(2,1)S(1)} %get-tuple-element.110), channel_id=1, source_target_pairs={{2,0},{4,2},{6,4},{8,6},{10,8},{12,10},{14,12},{16,14},{18,16},{20... | collective-permute-start | bytes 196616 | tf_op jit(solution)/shard_map/ppermute | solution.py:23
  14.3 0.9 fusion.22
  15.3 0.7 reshape.119
  16.0 0.7 copy.26
  17.0 0.9 pad_maximum_fusion
  18.0 102.8 %while.10 = (s32[]{:T(128)}, bf16[8,16,512]{2,1,0:T(8,128)(2,1)S(1)}, s32[8,16,128]{2,1,0:T(8,128)S(1)}, s32[8]{0:T(128)S(1)}, bf16[256,3]{0,1:T(4,128)(2,1)S(1)...) while((s32[]{:T(128)}, ...), condition=%wide.region_3.4_spmd, body=%wide.region_0.3_spmd.sunk | while | flops 392468480 | bytes 9009435 | solution.py:117
  18.0 0.6 dynamic_slice.48
  20.9 2.5 %fusion.52 = f32[16,128,512]{2,1,0:T(8,128)} fusion(s32[16,128]{1,0:T(8,128)S(1)} %subtract_bitcast_fusion.2, bf16[256,512]{1,0:T(8,128)(2,1)S(1)} %get-tuple-element.222, s32[]{:T(128)S(6)} %select_n.40), kind=kOutput, calls=%fused_computation.5.clone.1 | convolution fusion | flops 268697600 | bytes 4333572 | tf_op jit(solution)/shard_map/while/body/eval_jaxpr/dot_general | solution.py:47
  24.3 6.5 %multiply_reduce_fusion.5 = f32[16,512]{1,0:T(8,128)S(1)} fusion(f32[16,128,512]{2,1,0:T(8,128)} %fusion.52, f32[16,128]{1,0:T(8,128)S(1)} %fusion.54, f32[512]{0:T(512)S(1)} %copy-done.7, f32[16,128,3]{1,2,0:T(4,128)S(1)} %fusion.55, f32[16,128,6]{1,2,0:T(8,128)S(1)} %negate_exponential_fusion.2, f32[9,512]{1,0:T(8,128)S(1)} %copy-done.6), kind=kOutput, calls=%fused_computation.2.clone.1 | convolution fusion | flops 121645056 | bytes 4329472 | tf_op jit(solution)/shard_map/while/body/eval_jaxpr/bki,iw->bkw/dot_general | solution.py:37
  33.7 2.5 %fusion.52 = f32[16,128,512]{2,1,0:T(8,128)} fusion(s32[16,128]{1,0:T(8,128)S(1)} %subtract_bitcast_fusion.2, bf16[256,512]{1,0:T(8,128)(2,1)S(1)} %get-tuple-element.222, s32[]{:T(128)S(6)} %select_n.40), kind=kOutput, calls=%fused_computation.5.clone.1 | convolution fusion | flops 268697600 | bytes 4333572 | tf_op jit(solution)/shard_map/while/body/eval_jaxpr/dot_general | solution.py:47
  37.2 6.5 %multiply_reduce_fusion.5 = f32[16,512]{1,0:T(8,128)S(1)} fusion(f32[16,128,512]{2,1,0:T(8,128)} %fusion.52, f32[16,128]{1,0:T(8,128)S(1)} %fusion.54, f32[512]{0:T(512)S(1)} %copy-done.7, f32[16,128,3]{1,2,0:T(4,128)S(1)} %fusion.55, f32[16,128,6]{1,2,0:T(8,128)S(1)} %negate_exponential_fusion.2, f32[9,512]{1,0:T(8,128)S(1)} %copy-done.6), kind=kOutput, calls=%fused_computation.2.clone.1 | convolution fusion | flops 121645056 | bytes 4329472 | tf_op jit(solution)/shard_map/while/body/eval_jaxpr/bki,iw->bkw/dot_general | solution.py:37
  43.7 0.6 dynamic_slice.48
  46.5 2.5 %fusion.52 = f32[16,128,512]{2,1,0:T(8,128)} fusion(s32[16,128]{1,0:T(8,128)S(1)} %subtract_bitcast_fusion.2, bf16[256,512]{1,0:T(8,128)(2,1)S(1)} %get-tuple-element.222, s32[]{:T(128)S(6)} %select_n.40), kind=kOutput, calls=%fused_computation.5.clone.1 | convolution fusion | flops 268697600 | bytes 4333572 | tf_op jit(solution)/shard_map/while/body/eval_jaxpr/dot_general | solution.py:47
  50.0 6.5 %multiply_reduce_fusion.5 = f32[16,512]{1,0:T(8,128)S(1)} fusion(f32[16,128,512]{2,1,0:T(8,128)} %fusion.52, f32[16,128]{1,0:T(8,128)S(1)} %fusion.54, f32[512]{0:T(512)S(1)} %copy-done.7, f32[16,128,3]{1,2,0:T(4,128)S(1)} %fusion.55, f32[16,128,6]{1,2,0:T(8,128)S(1)} %negate_exponential_fusion.2, f32[9,512]{1,0:T(8,128)S(1)} %copy-done.6), kind=kOutput, calls=%fused_computation.2.clone.1 | convolution fusion | flops 121645056 | bytes 4329472 | tf_op jit(solution)/shard_map/while/body/eval_jaxpr/bki,iw->bkw/dot_general | solution.py:37
  59.4 2.5 %fusion.52 = f32[16,128,512]{2,1,0:T(8,128)} fusion(s32[16,128]{1,0:T(8,128)S(1)} %subtract_bitcast_fusion.2, bf16[256,512]{1,0:T(8,128)(2,1)S(1)} %get-tuple-element.222, s32[]{:T(128)S(6)} %select_n.40), kind=kOutput, calls=%fused_computation.5.clone.1 | convolution fusion | flops 268697600 | bytes 4333572 | tf_op jit(solution)/shard_map/while/body/eval_jaxpr/dot_general | solution.py:47
  62.9 6.5 %multiply_reduce_fusion.5 = f32[16,512]{1,0:T(8,128)S(1)} fusion(f32[16,128,512]{2,1,0:T(8,128)} %fusion.52, f32[16,128]{1,0:T(8,128)S(1)} %fusion.54, f32[512]{0:T(512)S(1)} %copy-done.7, f32[16,128,3]{1,2,0:T(4,128)S(1)} %fusion.55, f32[16,128,6]{1,2,0:T(8,128)S(1)} %negate_exponential_fusion.2, f32[9,512]{1,0:T(8,128)S(1)} %copy-done.6), kind=kOutput, calls=%fused_computation.2.clone.1 | convolution fusion | flops 121645056 | bytes 4329472 | tf_op jit(solution)/shard_map/while/body/eval_jaxpr/bki,iw->bkw/dot_general | solution.py:37
  72.2 2.5 %fusion.52 = f32[16,128,512]{2,1,0:T(8,128)} fusion(s32[16,128]{1,0:T(8,128)S(1)} %subtract_bitcast_fusion.2, bf16[256,512]{1,0:T(8,128)(2,1)S(1)} %get-tuple-element.222, s32[]{:T(128)S(6)} %select_n.40), kind=kOutput, calls=%fused_computation.5.clone.1 | convolution fusion | flops 268697600 | bytes 4333572 | tf_op jit(solution)/shard_map/while/body/eval_jaxpr/dot_general | solution.py:47
  75.7 6.5 %multiply_reduce_fusion.5 = f32[16,512]{1,0:T(8,128)S(1)} fusion(f32[16,128,512]{2,1,0:T(8,128)} %fusion.52, f32[16,128]{1,0:T(8,128)S(1)} %fusion.54, f32[512]{0:T(512)S(1)} %copy-done.7, f32[16,128,3]{1,2,0:T(4,128)S(1)} %fusion.55, f32[16,128,6]{1,2,0:T(8,128)S(1)} %negate_exponential_fusion.2, f32[9,512]{1,0:T(8,128)S(1)} %copy-done.6), kind=kOutput, calls=%fused_computation.2.clone.1 | convolution fusion | flops 121645056 | bytes 4329472 | tf_op jit(solution)/shard_map/while/body/eval_jaxpr/bki,iw->bkw/dot_general | solution.py:37
  82.3 0.6 dynamic_slice.48
  85.1 2.5 %fusion.52 = f32[16,128,512]{2,1,0:T(8,128)} fusion(s32[16,128]{1,0:T(8,128)S(1)} %subtract_bitcast_fusion.2, bf16[256,512]{1,0:T(8,128)(2,1)S(1)} %get-tuple-element.222, s32[]{:T(128)S(6)} %select_n.40), kind=kOutput, calls=%fused_computation.5.clone.1 | convolution fusion | flops 268697600 | bytes 4333572 | tf_op jit(solution)/shard_map/while/body/eval_jaxpr/dot_general | solution.py:47
  88.6 6.5 %multiply_reduce_fusion.5 = f32[16,512]{1,0:T(8,128)S(1)} fusion(f32[16,128,512]{2,1,0:T(8,128)} %fusion.52, f32[16,128]{1,0:T(8,128)S(1)} %fusion.54, f32[512]{0:T(512)S(1)} %copy-done.7, f32[16,128,3]{1,2,0:T(4,128)S(1)} %fusion.55, f32[16,128,6]{1,2,0:T(8,128)S(1)} %negate_exponential_fusion.2, f32[9,512]{1,0:T(8,128)S(1)} %copy-done.6), kind=kOutput, calls=%fused_computation.2.clone.1 | convolution fusion | flops 121645056 | bytes 4329472 | tf_op jit(solution)/shard_map/while/body/eval_jaxpr/bki,iw->bkw/dot_general | solution.py:37
  97.9 2.5 %fusion.52 = f32[16,128,512]{2,1,0:T(8,128)} fusion(s32[16,128]{1,0:T(8,128)S(1)} %subtract_bitcast_fusion.2, bf16[256,512]{1,0:T(8,128)(2,1)S(1)} %get-tuple-element.222, s32[]{:T(128)S(6)} %select_n.40), kind=kOutput, calls=%fused_computation.5.clone.1 | convolution fusion | flops 268697600 | bytes 4333572 | tf_op jit(solution)/shard_map/while/body/eval_jaxpr/dot_general | solution.py:47
  101.4 6.5 %multiply_reduce_fusion.5 = f32[16,512]{1,0:T(8,128)S(1)} fusion(f32[16,128,512]{2,1,0:T(8,128)} %fusion.52, f32[16,128]{1,0:T(8,128)S(1)} %fusion.54, f32[512]{0:T(512)S(1)} %copy-done.7, f32[16,128,3]{1,2,0:T(4,128)S(1)} %fusion.55, f32[16,128,6]{1,2,0:T(8,128)S(1)} %negate_exponential_fusion.2, f32[9,512]{1,0:T(8,128)S(1)} %copy-done.6), kind=kOutput, calls=%fused_computation.2.clone.1 | convolution fusion | flops 121645056 | bytes 4329472 | tf_op jit(solution)/shard_map/while/body/eval_jaxpr/bki,iw->bkw/dot_general | solution.py:37
  110.8 2.5 %fusion.52 = f32[16,128,512]{2,1,0:T(8,128)} fusion(s32[16,128]{1,0:T(8,128)S(1)} %subtract_bitcast_fusion.2, bf16[256,512]{1,0:T(8,128)(2,1)S(1)} %get-tuple-element.222, s32[]{:T(128)S(6)} %select_n.40), kind=kOutput, calls=%fused_computation.5.clone.1 | convolution fusion | flops 268697600 | bytes 4333572 | tf_op jit(solution)/shard_map/while/body/eval_jaxpr/dot_general | solution.py:47
  114.2 6.5 %multiply_reduce_fusion.5 = f32[16,512]{1,0:T(8,128)S(1)} fusion(f32[16,128,512]{2,1,0:T(8,128)} %fusion.52, f32[16,128]{1,0:T(8,128)S(1)} %fusion.54, f32[512]{0:T(512)S(1)} %copy-done.7, f32[16,128,3]{1,2,0:T(4,128)S(1)} %fusion.55, f32[16,128,6]{1,2,0:T(8,128)S(1)} %negate_exponential_fusion.2, f32[9,512]{1,0:T(8,128)S(1)} %copy-done.6), kind=kOutput, calls=%fused_computation.2.clone.1 | convolution fusion | flops 121645056 | bytes 4329472 | tf_op jit(solution)/shard_map/while/body/eval_jaxpr/bki,iw->bkw/dot_general | solution.py:37
  121.9 4.9 %psum.7 = f32[4,128]{1,0:T(4,128)S(1)} all-reduce(f32[4,128]{1,0:T(4,128)S(1)} %pad_maximum_fusion.2), channel_id=1, replica_groups=mesh['dom'=16,'frame'=2] {'frame'}, use_global_device_ids=true, to_apply=%region_4.5 | all-reduce | flops 512 | bytes 4096 | tf_op jit(solution)/shard_map/psum | solution.py:131
  126.8 0.6 broadcast_multiply_fusion
  (160 shorter events, 17.2 us)
Async XLA Ops:
  0.0 120.8 %copy-start = (bf16[512,512]{1,0:T(8,128)(2,1)S(1)}, bf16[512,512]{1,0:T(8,128)(2,1)}, u32[]{:S(2)}) copy-start(bf16[512,512]{1,0:T(8,128)(2,1)} %param.22) | copy-start | bytes 1572868
  2.4 14.4 %collective-permute-start = (bf16[64,3]{1,0:T(8,128)(2,1)S(1)}, bf16[64,3]{1,0:T(8,128)(2,1)S(1)}, u32[]{:S(2)}, u32[]{:S(2)}) collective-permute-start(bf16[64,3]{1,0:T(8,128)(2,1)S(1)} %get-tuple-element.111), channel_id=1, source_target_pairs={{0,2},{2,4},{4,6},{6,8},{8,10},{10,12},{12,14},{14,16},{16,18},{18... | collective-permute-start | bytes 1160 | tf_op jit(solution)/shard_map/ppermute | solution.py:21
  2.9 14.0 %collective-permute-start.1 = (bf16[64,3]{1,0:T(8,128)(2,1)S(1)}, bf16[64,3]{1,0:T(8,128)(2,1)S(1)}, u32[]{:S(2)}, u32[]{:S(2)}) collective-permute-start(bf16[64,3]{1,0:T(8,128)(2,1)S(1)} %get-tuple-element.112), channel_id=1, source_target_pairs={{2,0},{4,2},{6,4},{8,6},{10,8},{12,10},{14,12},{16,14},{18,16},{20... | collective-permute-start | bytes 1160 | tf_op jit(solution)/shard_map/ppermute | solution.py:23
  9.7 7.3 %collective-permute-start.2 = (bf16[64,512]{1,0:T(8,128)(2,1)S(1)}, bf16[64,512]{1,0:T(8,128)(2,1)S(1)}, u32[]{:S(2)}, u32[]{:S(2)}) collective-permute-start(bf16[64,512]{1,0:T(8,128)(2,1)S(1)} %get-tuple-element.109), channel_id=1, source_target_pairs={{0,2},{2,4},{4,6},{6,8},{8,10},{10,12},{12,14},{14,16},{16,18},{18... | collective-permute-start | bytes 196616 | tf_op jit(solution)/shard_map/ppermute | solution.py:21
  9.8 7.2 %collective-permute-start.3 = (bf16[64,512]{1,0:T(8,128)(2,1)S(1)}, bf16[64,512]{1,0:T(8,128)(2,1)S(1)}, u32[]{:S(2)}, u32[]{:S(2)}) collective-permute-start(bf16[64,512]{1,0:T(8,128)(2,1)S(1)} %get-tuple-element.110), channel_id=1, source_target_pairs={{2,0},{4,2},{6,4},{8,6},{10,8},{12,10},{14,12},{16,14},{18,16},{20... | collective-permute-start | bytes 196616 | tf_op jit(solution)/shard_map/ppermute | solution.py:23
  17.9 103.1 %copy-start.1 = (bf16[128,512]{1,0:T(8,128)(2,1)S(1)}, bf16[128,512]{1,0:T(8,128)(2,1)}, u32[]{:S(2)}) copy-start(bf16[128,512]{1,0:T(8,128)(2,1)} %param.14) | copy-start | bytes 393220
  18.0 103.1 %copy-start.4 = (bf16[512,512]{1,0:T(8,128)(2,1)S(1)}, bf16[512,512]{1,0:T(8,128)(2,1)}, u32[]{:S(2)}) copy-start(bf16[512,512]{1,0:T(8,128)(2,1)} %param.24) | copy-start | bytes 1572868
  18.0 103.1 %copy-start.5 = (bf16[512,512]{1,0:T(8,128)(2,1)S(1)}, bf16[512,512]{1,0:T(8,128)(2,1)}, u32[]{:S(2)}) copy-start(bf16[512,512]{1,0:T(8,128)(2,1)} %param.23) | copy-start | bytes 1572868
  18.0 6.3 %copy-start.6 = (f32[9,512]{1,0:T(8,128)S(1)}, f32[9,512]{1,0:T(8,128)}, u32[]{:S(2)}) copy-start(f32[9,512]{1,0:T(8,128)} %get-tuple-element.219) | copy-start | bytes 55300 | tf_op jit(solution)/shard_map/while
  18.0 6.3 %copy-start.7 = (f32[512]{0:T(512)S(1)}, f32[512]{0:T(512)}, u32[]{:S(2)}) copy-start(f32[512]{0:T(512)} %get-tuple-element.220) | copy-start | bytes 6148 | tf_op jit(solution)/shard_map/while
  30.8 6.3 %copy-start.6 = (f32[9,512]{1,0:T(8,128)S(1)}, f32[9,512]{1,0:T(8,128)}, u32[]{:S(2)}) copy-start(f32[9,512]{1,0:T(8,128)} %get-tuple-element.219) | copy-start | bytes 55300 | tf_op jit(solution)/shard_map/while
  30.8 6.3 %copy-start.7 = (f32[512]{0:T(512)S(1)}, f32[512]{0:T(512)}, u32[]{:S(2)}) copy-start(f32[512]{0:T(512)} %get-tuple-element.220) | copy-start | bytes 6148 | tf_op jit(solution)/shard_map/while
  43.7 6.3 %copy-start.6 = (f32[9,512]{1,0:T(8,128)S(1)}, f32[9,512]{1,0:T(8,128)}, u32[]{:S(2)}) copy-start(f32[9,512]{1,0:T(8,128)} %get-tuple-element.219) | copy-start | bytes 55300 | tf_op jit(solution)/shard_map/while
  43.7 6.3 %copy-start.7 = (f32[512]{0:T(512)S(1)}, f32[512]{0:T(512)}, u32[]{:S(2)}) copy-start(f32[512]{0:T(512)} %get-tuple-element.220) | copy-start | bytes 6148 | tf_op jit(solution)/shard_map/while
  56.5 6.3 %copy-start.6 = (f32[9,512]{1,0:T(8,128)S(1)}, f32[9,512]{1,0:T(8,128)}, u32[]{:S(2)}) copy-start(f32[9,512]{1,0:T(8,128)} %get-tuple-element.219) | copy-start | bytes 55300 | tf_op jit(solution)/shard_map/while
  56.5 6.3 %copy-start.7 = (f32[512]{0:T(512)S(1)}, f32[512]{0:T(512)}, u32[]{:S(2)}) copy-start(f32[512]{0:T(512)} %get-tuple-element.220) | copy-start | bytes 6148 | tf_op jit(solution)/shard_map/while
  69.4 6.3 %copy-start.6 = (f32[9,512]{1,0:T(8,128)S(1)}, f32[9,512]{1,0:T(8,128)}, u32[]{:S(2)}) copy-start(f32[9,512]{1,0:T(8,128)} %get-tuple-element.219) | copy-start | bytes 55300 | tf_op jit(solution)/shard_map/while
  69.4 6.3 %copy-start.7 = (f32[512]{0:T(512)S(1)}, f32[512]{0:T(512)}, u32[]{:S(2)}) copy-start(f32[512]{0:T(512)} %get-tuple-element.220) | copy-start | bytes 6148 | tf_op jit(solution)/shard_map/while
  82.2 6.3 %copy-start.6 = (f32[9,512]{1,0:T(8,128)S(1)}, f32[9,512]{1,0:T(8,128)}, u32[]{:S(2)}) copy-start(f32[9,512]{1,0:T(8,128)} %get-tuple-element.219) | copy-start | bytes 55300 | tf_op jit(solution)/shard_map/while
  82.2 6.3 %copy-start.7 = (f32[512]{0:T(512)S(1)}, f32[512]{0:T(512)}, u32[]{:S(2)}) copy-start(f32[512]{0:T(512)} %get-tuple-element.220) | copy-start | bytes 6148 | tf_op jit(solution)/shard_map/while
  95.1 6.3 %copy-start.6 = (f32[9,512]{1,0:T(8,128)S(1)}, f32[9,512]{1,0:T(8,128)}, u32[]{:S(2)}) copy-start(f32[9,512]{1,0:T(8,128)} %get-tuple-element.219) | copy-start | bytes 55300 | tf_op jit(solution)/shard_map/while
  95.1 6.3 %copy-start.7 = (f32[512]{0:T(512)S(1)}, f32[512]{0:T(512)}, u32[]{:S(2)}) copy-start(f32[512]{0:T(512)} %get-tuple-element.220) | copy-start | bytes 6148 | tf_op jit(solution)/shard_map/while
  107.9 6.3 %copy-start.6 = (f32[9,512]{1,0:T(8,128)S(1)}, f32[9,512]{1,0:T(8,128)}, u32[]{:S(2)}) copy-start(f32[9,512]{1,0:T(8,128)} %get-tuple-element.219) | copy-start | bytes 55300 | tf_op jit(solution)/shard_map/while
  107.9 6.3 %copy-start.7 = (f32[512]{0:T(512)S(1)}, f32[512]{0:T(512)}, u32[]{:S(2)}) copy-start(f32[512]{0:T(512)} %get-tuple-element.220) | copy-start | bytes 6148 | tf_op jit(solution)/shard_map/while
  120.8 0.8 copy-start.2
  120.8 0.9 copy-start.3
where the time goes:
time: 128 us; the launch traced here: 127 us
  matrix products  78 us (61%)
  loops' own time  14.2 us (11%)
  local copies, waits for them, and re-layouts  11.5 us (9%)
  starting transfers between devices  10 us (8%)
  other arithmetic  8.51 us (7%)
  blocking collectives  4.94 us (4%)
    dot_general x8, matrix products, edge_messages(): jnp.einsum('bki,iw->bkw', edge_in, w_edge, precision=lax.Precision.HIGHEST)  51.8 us
    dot_general x8, matrix products, fetch_rows(): jnp.dot(flat_pick, window_feat, preferred_element_type=jnp.float32)  19.9 us
    another operation x1, loops' own time, local(): lax.map(one_block, block_inputs).reshape(local_atoms, feature_width)  14.2 us
    ppermute x2, starting transfers between devices, padded(): lax.ppermute(head, axis, [((i + 1) % count, i) for i in range(count)])  9.46 us
    psum x1, blocking collectives, local(): return lax.psum(frame_term, 'frame') / frame_count  4.94 us
    dynamic_slice x8, local copies, waits for them, and re-layouts, local(): lax.map(one_block, block_inputs).reshape(local_atoms, feature_width)  4.66 us
    sub x8, other arithmetic, one_block(): local_rows = block_idx - block_start  4.53 us
    dot_general x8, matrix products, fetch_rows(): got_pos = jnp.dot(flat_pick, window_pos, preferred_element_type=jnp.float32)  3.73 us
  transfers between devices with their start and end apart: 4, of which 0 were waited for; matrix products, arithmetic and copies ran while one was open for 4% of the time, Pallas kernels for 0%

commit v1 on v0

v1 whole, which is shorter than its diff:
```python
import functools

import jax
import jax.numpy as jnp
from jax import lax
from jax.experimental import pallas as pl
from jax.experimental.pallas import tpu as pltpu
from jax.sharding import PartitionSpec as P

F32 = jnp.float32
BF16 = jnp.bfloat16
MESH = pl.DeviceIdType.MESH
WINDOW = 128
message_scale = 0.0884
radial_step = 1.25
block_atoms = 16
UNROLL = 2


def iota(shape, dim):
    return lax.broadcasted_iota(jnp.int32, shape, dim)


def dot(a, b):
    return jnp.dot(a, b, preferred_element_type=F32)


def split(value):
    high = value.astype(BF16).astype(F32)
    return high, value - high


def silu(x):
    half = 0.5 * x
    return half + half * jnp.tanh(half)


def up16(n):
    return (n + 15) // 16 * 16


def chunk_sizes(F, atoms, cap):
    blocks = atoms // block_atoms
    per = blocks // F
    span = atoms + 2 * cap - WINDOW
    own, ghost = [0] * per, [0] * per
    for f in range(F):
        for b in range(f * per, (f + 1) * per):
            start = b * span // max(blocks - 1, 1)
            low, high = max(start - cap, 0), min(start + WINDOW - cap, atoms)
            below, above = max(cap - start, 0), max(start + WINDOW - cap - atoms, 0)
            if f < F // 2:
                assert above == 0
                l, need, gh = b - f * per, high, below
            else:
                assert below == 0
                l, need, gh = (f + 1) * per - 1 - b, atoms - low, above
            own[l] = max(own[l], up16(need))
            ghost[l] = max(ghost[l], up16(gh))
    return own, ghost


def kernel(
    F, D, atoms, cap, width,
    feat, pos, nbr, cnt, send, frames, w_edge, b_edge, w_msg_h, w_upd_h, w_read_h, w_heads,
    out,
    table, cols, nbr_s, add_s, own_u, send_buf, ghost_buf, lhs, fr_stage, fr_s, base_s, wst,
    msg_s, z_s, fin_stage, fin_s, w_msg, w_upd, w_read,
    w_sem, halo_send, halo_recv, fr_send, fr_recv, fin_send, fin_recv,
):
    f = lax.axis_index("frame")
    d = lax.axis_index("dom")
    side = f // (F // 2)
    blocks = atoms // block_atoms
    per = blocks // F
    nat = per * block_atoms
    own_n, ghost_n = chunk_sizes(F, atoms, cap)
    region = atoms + cap
    first = f * nat

    barrier = pltpu.get_barrier_semaphore()
    peers = [lax.rem(f + k, F) for k in range(1, F)]
    up, down = lax.rem(d + 1, D), lax.rem(d + D - 1, D)
    for peer in peers:
        pl.semaphore_signal(barrier, inc=1, device_id={"frame": peer}, device_id_type=MESH)
    for near in (up, down):
        pl.semaphore_signal(barrier, inc=1, device_id={"dom": near}, device_id_type=MESH)
    weight_copies = [
        pltpu.make_async_copy(src, dst, w_sem.at[n])
        for n, (src, dst) in enumerate(((w_msg_h, w_msg), (w_upd_h, w_upd), (w_read_h, w_read)))
    ]
    for copy in weight_copies:
        copy.start()

    lane = iota((128, 128), 1)
    row = iota((128, 128), 0)

    table[...] = jnp.zeros_like(table)
    table[0:3, :] = pos[...].astype(F32)
    table[3:4, :] = cnt[...].astype(F32)
    by_atom = table[...].T
    sq = jnp.sum(jnp.where(lane < 3, by_atom * by_atom, 0.0), axis=1, keepdims=True)
    sq_hi, rest = split(sq)
    sq_mid, sq_lo = split(rest)
    u = jnp.where(lane < 3, by_atom, 0.0)
    u = jnp.where(lane == 3, sq_hi, u)
    u = jnp.where(lane == 4, sq_mid, u)
    u = jnp.where(lane == 5, sq_lo, u)
    u = jnp.where((lane >= 6) & (lane < 9), 1.0, u)
    own_u[...] = u.astype(BF16)

    fr_stage[...] = jnp.zeros_like(fr_stage)
    for a in range(3):
        fr_stage[a : a + 1, 0:3] = frames[a]
    fr_s[f] = fr_stage[...]
    chosen = jnp.where(side == 0, send[1:2, :], send[0:1, :])
    pick = (iota((atoms, cap), 0) == chosen).astype(F32).T.astype(BF16)
    send_buf[:, 0:width] = dot(pick, feat[...]).astype(BF16)
    send_buf[:, width : width + 128] = dot(pick, own_u[...]).astype(BF16)

    pl.semaphore_wait(barrier, F + 1)
    target = jnp.where(side == 0, up, down)
    halo = pltpu.make_async_remote_copy(
        src_ref=send_buf, dst_ref=ghost_buf, send_sem=halo_send, recv_sem=halo_recv,
        device_id={"dom": target}, device_id_type=MESH,
    )
    fr_copies = [
        pltpu.make_async_remote_copy(
            src_ref=fr_stage, dst_ref=fr_s.at[f], send_sem=fr_send.at[k], recv_sem=fr_recv.at[k],
            device_id={"frame": peer}, device_id_type=MESH,
        )
        for k, peer in enumerate(peers)
    ]
    for copy in fr_copies:
        copy.start()
    halo.start()

    live = iota((atoms, nbr.shape[1]), 1).astype(F32) < by_atom[:, 3:4]
    nbr_s[...] = jnp.where(live, nbr[...].astype(F32), -1.0)

    radial = lane % 8
    spot = (lane // 8) * 2 + radial - 6
    special = radial >= 6
    place = special & (spot < 6) & (row < 3) & (row == spot % 3)
    place_neg = special & (spot >= 6) & (spot < 12) & (row < 3) & (row == spot % 3)
    place_one = special & (spot >= 12) & (spot < 14) & (row == 6)
    place_add = jnp.where(place_one, 1.0, jnp.where(place_neg, -1.0, 0.0)).astype(BF16)
    add_s[...] = dot(own_u[...], place_add)
    place = jnp.where(place, 1.0, 0.0).astype(BF16)
    centres = radial[0:1, :].astype(F32) * radial_step

    def block_rows(l):
        return (l * (1 - side) + (per - 1 - l) * side) * block_atoms

    def own_base(l):
        return pl.multiple_of(side * (atoms - own_n[l]), 16)

    def ghost_base(l):
        return pl.multiple_of((1 - side) * (cap - ghost_n[l]), 16)

    def geometry(l):
        start = first + block_rows(l)
        expand = jnp.where(row == start + lane // 8, 1.0, 0.0).astype(BF16)
        centre = dot(table[0:16, :].astype(BF16), expand)
        sub = iota((16, 128), 0)
        sqi = jnp.sum(jnp.where(sub < 3, centre * centre, 0.0), axis=0, keepdims=True) + 0.25
        hi, tail = split(sqi)
        mid, lo = split(tail)
        g = jnp.where((row >= 3) & (row < 6), 1.0, 0.0)
        for c in range(3):
            g = jnp.where(row == c, -2.0 * centre[c : c + 1, :], g)
        for c, part in enumerate((hi, mid, lo)):
            g = jnp.where(row == 6 + c, part, g)
        return g.astype(BF16)

    def fill(l, g, rows_u, offset):
        n = rows_u.shape[0]
        d2 = dot(rows_u, g)
        placed = dot(rows_u, place)
        dist = jnp.sqrt(jnp.maximum(d2, 0.25))
        gap = dist - centres
        value = jnp.exp(-(gap * gap))
        spec = special[0:n, :]
        lhs[l * region + offset : l * region + offset + n, 0:128] = jnp.where(spec, 0.0, value).astype(BF16)
        lhs[l * region + offset : l * region + offset + n, 128:256] = jnp.where(spec, placed, value).astype(BF16)

    gs = []
    for l in range(per):
        g = geometry(l)
        gs.append(g)
        fill(l, g, own_u[pl.ds(own_base(l), own_n[l]), :], 0)

    r = iota((256, 32), 0)
    c = iota((256, 32), 1)
    rb = r % 8
    rs = (r % 128) // 8 * 2 + rb - 6
    second = r // 128
    want = jnp.where(rb < 6, second * 6 + rb, -1)
    sp = (rb >= 6) & (second == 1)
    want = jnp.where(sp & (rs < 3), 12 + rs, want)
    want = jnp.where(sp & (rs >= 3) & (rs < 6), 12 + rs, want)
    want = jnp.where(sp & (rs >= 6) & (rs < 12), 6 + rs, want)
    want = jnp.where(sp & (rs >= 12) & (rs < 14), 6 + rs, want)
    sel = jnp.where(want == c, 1.0, 0.0).astype(BF16)
    base_s[...] = jnp.zeros_like(base_s)
    hi, lo = split(0.5 * w_edge[0:6, :])
    base_s[0:6, :] = hi
    base_s[6:12, :] = lo
    hi, lo = split(0.5 * b_edge[...])
    base_s[18:19, :] = hi
    base_s[19:20, :] = lo
    for copy in fr_copies:
        copy.wait()
    for fr in range(F):
        for cc in range(3):
            acc = fr_s[fr, 0:1, cc : cc + 1] * w_edge[6:7, :]
            acc = acc + fr_s[fr, 1:2, cc : cc + 1] * w_edge[7:8, :]
            acc = acc + fr_s[fr, 2:3, cc : cc + 1] * w_edge[8:9, :]
            hi, lo = split(0.5 * acc)
            base_s[12 + cc : 13 + cc, :] = hi
            base_s[15 + cc : 16 + cc, :] = lo
        wst[:, fr * width : (fr + 1) * width] = dot(sel, base_s[...].astype(BF16)).astype(BF16)

    lane1 = iota((1, 128), 1)
    group = lane1 // 8
    special1 = lane1 % 8 >= 6

    def atom(l, i, n, offset, first_id, load_feat, add):
        local = block_rows(l) + i
        ids = (first_id + iota((n, 128), 0)).astype(F32)
        named = nbr_s[pl.ds(first + local, 1), :]
        mult = jnp.sum(jnp.where(ids == named, 1.0, 0.0), axis=1, keepdims=True)
        weighted = load_feat() * mult.astype(BF16)
        mask = jnp.where((group == i) & (~special1), 1.0, 0.0)
        extra = add_s[pl.ds(first + local, 1), :]
        left1 = lhs[l * region + offset : l * region + offset + n, 0:128] * mask.astype(BF16)
        left2 = lhs[l * region + offset : l * region + offset + n, 128:256]
        left2 = left2 * jnp.where(special1, 1.0, mask).astype(BF16) + extra.astype(BF16)
        left = jnp.concatenate([left1, left2], axis=1)
        for fr in range(F):
            h = dot(left, wst[:, fr * width : (fr + 1) * width]).astype(BF16)
            terms = (h + h * jnp.tanh(h)) * weighted
            parts = [terms[k : k + 16, :] for k in range(0, n, 16)]
            while len(parts) > 1:
                parts = [sum(parts[k + 1 : k + 2], parts[k]) for k in range(0, len(parts), 2)]
            total = jnp.sum(parts[0].astype(F32), axis=0, keepdims=True)
            spot = pl.ds(fr * nat + local, 1)
            if add:
                msg_s[spot, :] = msg_s[spot, :] + total
            else:
                msg_s[spot, :] = total

    def sweep(l, n, offset, first_id, load_feat, add):
        def step(k, _):
            for j in range(UNROLL):
                atom(l, k * UNROLL + j, n, offset, first_id, load_feat, add)
            return 0

        lax.fori_loop(0, block_atoms // UNROLL, step, 0)

    for l in range(per):
        base = own_base(l)
        sweep(l, own_n[l], 0, base, lambda l=l, base=base: feat[pl.ds(base, own_n[l]), :], False)

    halo.wait()
    for l in range(per):
        if ghost_n[l] == 0:
            continue
        base = ghost_base(l)
        fill(l, gs[l], ghost_buf[pl.ds(base, ghost_n[l]), width : width + 128], atoms)
        sweep(
            l, ghost_n[l], atoms, atoms + side * cap + base,
            lambda l=l, base=base: ghost_buf[pl.ds(base, ghost_n[l]), 0:width], True,
        )

    for copy in weight_copies:
        copy.wait()
    message = (msg_s[...] * message_scale).astype(BF16)
    hidden = silu(dot(message, w_msg[...])).astype(BF16)
    own = feat[pl.ds(pl.multiple_of(first, 16), nat), :].astype(F32)
    updated = (jnp.concatenate([own] * F, axis=0) + dot(hidden, w_upd[...])).astype(BF16)
    readout = silu(dot(updated, w_read[...])).astype(BF16)
    heads = lax.dot_general(w_heads[...], readout, (((1,), (1,)), ((), ())), preferred_element_type=F32)
    segment = lane1 // nat
    z_s[...] = jnp.zeros_like(z_s)
    for cc in range(3):
        total = jnp.zeros((1, 128), F32)
        for a in range(3):
            rot = jnp.zeros((1, 128), F32)
            for fr in range(F):
                rot = jnp.where(segment == fr, fr_s[fr, a : a + 1, cc : cc + 1], rot)
            total = total + rot * heads[a : a + 1, :]
        z_s[cc : cc + 1, :] = total
    z_s[3:4, :] = heads[3:4, :]
    z = z_s[...]
    total = z
    for k in range(1, F):
        total = total + pltpu.roll(z, k * nat, 1)
    fin_stage[...] = jnp.where(segment == f, total / F, 0.0)
    fin_copies = [
        pltpu.make_async_remote_copy(
            src_ref=fin_stage, dst_ref=fin_s.at[k], send_sem=fin_send.at[k], recv_sem=fin_recv.at[k],
            device_id={"frame": peer}, device_id_type=MESH,
        )
        for k, peer in enumerate(peers)
    ]
    for copy in fin_copies:
        copy.start()
    result = fin_stage[...]
    for k, copy in enumerate(fin_copies):
        copy.wait()
        result = result + fin_s[k]
    out[...] = result[0:4, :]


def local(F, D, features, positions, neighbours, counts, send_rows, frames, w_edge, b_edge,
          w_message, w_update, w_readout, w_heads):
    atoms, width = features.shape
    cap = send_rows.shape[2]
    slots = neighbours.shape[1]
    per = atoms // block_atoms // F
    vmem = pl.BlockSpec(memory_space=pltpu.VMEM)
    hbm = pl.BlockSpec(memory_space=pl.ANY)
    dma = pltpu.SemaphoreType.DMA
    return pl.pallas_call(
        functools.partial(kernel, F, D, atoms, cap, width),
        out_shape=jax.ShapeDtypeStruct((4, atoms), F32),
        in_specs=[vmem] * 8 + [hbm] * 3 + [vmem],
        out_specs=vmem,
        scratch_shapes=[
            pltpu.VMEM((128, atoms), F32),
            pltpu.VMEM((8, 128), F32),
            pltpu.VMEM((atoms, slots), F32),
            pltpu.VMEM((atoms, 128), F32),
            pltpu.VMEM((atoms, 128), BF16),
            pltpu.VMEM((cap, width + 128), BF16),
            pltpu.VMEM((cap, width + 128), BF16),
            pltpu.VMEM((per * (atoms + cap), 256), BF16),
            pltpu.VMEM((8, 128), F32),
            pltpu.VMEM((F, 8, 128), F32),
            pltpu.VMEM((32, width), F32),
            pltpu.VMEM((256, F * width), BF16),
            pltpu.VMEM((F * per * block_atoms, width), F32),
            pltpu.VMEM((8, 128), F32),
            pltpu.VMEM((8, 128), F32),
            pltpu.VMEM((F, 8, 128), F32),
            pltpu.VMEM((width, width), BF16),
            pltpu.VMEM((width, width), BF16),
            pltpu.VMEM((width, width), BF16),
            dma((3,)),
            dma,
            dma,
            dma((F - 1,)),
            dma((F - 1,)),
            dma((F - 1,)),
            dma((F - 1,)),
        ],
        compiler_params=pltpu.CompilerParams(
            collective_id=0, has_side_effects=True, vmem_limit_bytes=48 * 1024 * 1024
        ),
    )(
        features, positions, neighbours, counts.reshape(1, -1), send_rows.reshape(2, cap),
        frames.transpose(1, 0, 2), w_edge, b_edge.reshape(1, -1), w_message, w_update, w_readout,
        w_heads.T,
    )


def solution(mesh):
    placed = (
        P("dom", None),
        P(None, "dom"),
        P("dom", None),
        P("dom"),
        P("dom", None, None),
        P("frame", None, None),
        P(),
        P(),
        P(),
        P(),
        P(),
        P(),
    )
    body = functools.partial(local, mesh.shape["frame"], mesh.shape["dom"])
    return jax.shard_map(
        body, mesh=mesh, in_specs=placed, out_specs=P(None, "dom"), check_vma=False
    )
```

time: 128 us -> 41.8 us (0.33)
  matrix products: 78 us -> 0 us
  Pallas kernels: 0 us -> 33.7 us
  loops' own time: 14.2 us -> 0 us
  starting transfers between devices: 10 us -> 0 us
  other arithmetic: 8.51 us -> 0 us
  blocking collectives: 4.94 us -> 0 us
  local copies, waits for them, and re-layouts: 11.5 us -> 7.62 us
    dot_general x36 -> x0, matrix products: 78 us -> none  [the longest x8 51.8 us: edge_messages(): jnp.einsum('bki,iw->bkw', edge_in, w_edge, precision=lax.Precision.HIGHEST)]
    pallas_call x0 -> x1, Pallas kernels: none -> 33.7 us  [local(): pl.pallas_call(functools.partial(kernel, F, D, atoms, cap, width), out_sh...]
    another operation x1 -> x0, loops' own time: 14.2 us -> none  [local(): lax.map(one_block, block_inputs).reshape(local_atoms, feature_width)]
    ppermute x4 -> x0, starting transfers between devices: 10 us -> none  [the longest x2 9.46 us: padded(): lax.ppermute(head, axis, [((i + 1) % count, i) for i in range(count)])]
    unnamed x14 -> x25, local copies, waits for them, and re-layouts: 1.59 us -> 7.62 us
    psum x1 -> x0, blocking collectives: 4.94 us -> none  [local(): return lax.psum(frame_term, 'frame') / frame_count]
    dynamic_slice x8 -> x0, local copies, waits for them, and re-layouts: 4.66 us -> none  [local(): lax.map(one_block, block_inputs).reshape(local_atoms, feature_width)]
    sub x8 -> x0, other arithmetic: 4.53 us -> none  [one_block(): local_rows = block_idx - block_start]
  transfers between devices with their start and end apart: 4 -> 0, of which waited for: 0 -> 0; matrix products, arithmetic and copies ran while one was open for 4% -> 0% of each run, Pallas kernels for 0% -> 0%
where the time goes in v1:
time: 41.8 us; the launch traced here: 41.4 us
  Pallas kernels  33.7 us (81%)
  local copies, waits for them, and re-layouts  7.62 us (18%)
    pallas_call x1, Pallas kernels, local(): pl.pallas_call(functools.partial(kernel, F, D, atoms, cap, width), out_sh...  33.7 us
    unnamed x25, local copies, waits for them, and re-layouts  7.62 us

profile of v1, /device:TPU:0, one launch (start us, length us, event | category | flops | bytes accessed | tf_op | source)
XLA Modules:
  0.0 41.4 jit_solution(11080201012415581743)
XLA Ops:
  0.0 0.0 copy-start.9
  0.0 0.0 copy-start.11
  0.0 0.0 copy-start.6
  0.0 0.0 copy-start.7
  0.0 0.0 copy-start.8
  0.0 0.7 %copy-done.9 = bf16[3,128]{1,0:T(4,128)(2,1)S(1)} copy-done((bf16[3,128]{1,0:T(4,128)(2,1)S(1)}, bf16[3,128]{1,0:T(4,128)(2,1)}, u32[]{:S(2)}) %copy-start.9) | copy-done | bytes 792
  0.7 0.0 copy-done.11
  0.7 0.0 copy-done.6
  0.7 0.0 copy-done.7
  0.7 0.0 copy-done.8
  0.7 0.0 copy-start
  0.7 1.0 %copy-done = bf16[512,512]{1,0:T(8,128)(2,1)S(1)} copy-done((bf16[512,512]{1,0:T(8,128)(2,1)S(1)}, bf16[512,512]{1,0:T(8,128)(2,1)}, u32[]{:S(2)}) %copy-start) | copy-done | bytes 524312
  1.8 0.0 copy-start.1
  1.8 1.0 %copy-done.1 = bf16[512,512]{1,0:T(8,128)(2,1)S(1)} copy-done((bf16[512,512]{1,0:T(8,128)(2,1)S(1)}, bf16[512,512]{1,0:T(8,128)(2,1)}, u32[]{:S(2)}) %copy-start.1) | copy-done | bytes 524312
  2.8 0.0 copy-start.2
  2.8 1.0 %copy-done.2 = bf16[512,512]{1,0:T(8,128)(2,1)S(1)} copy-done((bf16[512,512]{1,0:T(8,128)(2,1)S(1)}, bf16[512,512]{1,0:T(8,128)(2,1)}, u32[]{:S(2)}) %copy-start.2) | copy-done | bytes 524312
  3.9 0.0 copy-start.3
  3.9 0.9 %copy-done.3 = bf16[128,512]{1,0:T(8,128)(2,1)S(1)} copy-done((bf16[128,512]{1,0:T(8,128)(2,1)S(1)}, bf16[128,512]{1,0:T(8,128)(2,1)}, u32[]{:S(2)}) %copy-start.3) | copy-done | bytes 131096
  4.8 0.0 copy-start.4
  4.8 0.8 %copy-done.4 = s32[128,128]{1,0:T(8,128)S(1)} copy-done((s32[128,128]{1,0:T(8,128)S(1)}, s32[128,128]{1,0:T(8,128)}, u32[]{:S(2)}) %copy-start.4) | copy-done | bytes 65560
  5.6 0.0 copy-start.5
  5.6 0.8 %copy-done.5 = f32[9,512]{1,0:T(8,128)S(1)} copy-done((f32[9,512]{1,0:T(8,128)S(1)}, f32[9,512]{1,0:T(8,128)}, u32[]{:S(2)}) %copy-start.5) | copy-done | bytes 18456
  6.4 0.0 copy-start.10
  6.4 0.7 %copy-done.10 = s32[1,2,64]{2,1,0:T(2,128)S(1)} copy-done((s32[1,2,64]{2,1,0:T(2,128)S(1)}, s32[1,2,64]{2,1,0:T(2,128)}, u32[]{:S(2)}) %copy-start.10) | copy-done | bytes 536
  7.1 33.7 %shard_map.118 = f32[4,128]{1,0:T(4,128)S(1)} custom-call(bf16[128,512]{1,0:T(8,128)(2,1)S(1)} %copy-done.3, bf16[3,128]{1,0:T(4,128)(2,1)S(1)} %copy-done.9, s32[128,128]{1,0:T(8,128)S(1)} %copy-done.4, s32[1,128]{1,0:T(1,128)S(1)} %bitcast.9, s32[2,64]{1,0:T(2,128)S(1)} %bitcast.8, f32[3,1,3]{2,1,0:T(1,128)S(1)} %bitcast.7, f32[9,512]{1,0:T(8,128)S(1)} %copy-done.5, ...), custom_call_target="tpu_custom_call" | custom-call | tf_op jit(solution)/shard_map/pallas_call | solution.py:325
  40.8 0.6 %copy.14 = f32[4,128]{1,0:T(4,128)} copy(f32[4,128]{1,0:T(4,128)S(1)} %shard_map.118) | data formatting | bytes 4096
Async XLA Ops:
  0.0 0.7 %copy-start.9 = (bf16[3,128]{1,0:T(4,128)(2,1)S(1)}, bf16[3,128]{1,0:T(4,128)(2,1)}, u32[]{:S(2)}) copy-start(bf16[3,128]{1,0:T(4,128)(2,1)} %pos.1) | copy-start | bytes 2308
  0.0 0.7 %copy-start.11 = (s32[128]{0:T(128)S(1)}, s32[128]{0:T(128)}, u32[]{:S(2)}) copy-start(s32[128]{0:T(128)} %param.15) | copy-start | bytes 1540
  0.0 0.7 %copy-start.6 = (bf16[512,4]{0,1:T(4,128)(2,1)S(1)}, bf16[512,4]{0,1:T(4,128)(2,1)}, u32[]{:S(2)}) copy-start(bf16[512,4]{0,1:T(4,128)(2,1)} %param.23) | copy-start | bytes 12292
  0.0 0.7 %copy-start.7 = (f32[512]{0:T(512)S(1)}, f32[512]{0:T(512)}, u32[]{:S(2)}) copy-start(f32[512]{0:T(512)} %param.19) | copy-start | bytes 6148
  0.0 0.7 %copy-start.8 = (f32[1,3,3]{2,0,1:T(1,128)S(1)}, f32[1,3,3]{2,0,1:T(1,128)}, u32[]{:S(2)}) copy-start(f32[1,3,3]{2,0,1:T(1,128)} %param.17) | copy-start | bytes 112
  0.7 1.0 %copy-start = (bf16[512,512]{1,0:T(8,128)(2,1)S(1)}, bf16[512,512]{1,0:T(8,128)(2,1)}, u32[]{:S(2)}) copy-start(bf16[512,512]{1,0:T(8,128)(2,1)} %w_msg_h.1) | copy-start | bytes 1572868
  1.8 1.0 %copy-start.1 = (bf16[512,512]{1,0:T(8,128)(2,1)S(1)}, bf16[512,512]{1,0:T(8,128)(2,1)}, u32[]{:S(2)}) copy-start(bf16[512,512]{1,0:T(8,128)(2,1)} %w_upd_h.1) | copy-start | bytes 1572868
  2.8 1.0 %copy-start.2 = (bf16[512,512]{1,0:T(8,128)(2,1)S(1)}, bf16[512,512]{1,0:T(8,128)(2,1)}, u32[]{:S(2)}) copy-start(bf16[512,512]{1,0:T(8,128)(2,1)} %w_read_h.1) | copy-start | bytes 1572868
  3.9 0.9 %copy-start.3 = (bf16[128,512]{1,0:T(8,128)(2,1)S(1)}, bf16[128,512]{1,0:T(8,128)(2,1)}, u32[]{:S(2)}) copy-start(bf16[128,512]{1,0:T(8,128)(2,1)} %feat.1) | copy-start | bytes 393220
  4.8 0.8 %copy-start.4 = (s32[128,128]{1,0:T(8,128)S(1)}, s32[128,128]{1,0:T(8,128)}, u32[]{:S(2)}) copy-start(s32[128,128]{1,0:T(8,128)} %nbr.1) | copy-start | bytes 196612
  5.6 0.8 %copy-start.5 = (f32[9,512]{1,0:T(8,128)S(1)}, f32[9,512]{1,0:T(8,128)}, u32[]{:S(2)}) copy-start(f32[9,512]{1,0:T(8,128)} %w_edge.1) | copy-start | bytes 55300
  6.4 0.7 %copy-start.10 = (s32[1,2,64]{2,1,0:T(2,128)S(1)}, s32[1,2,64]{2,1,0:T(2,128)}, u32[]{:S(2)}) copy-start(s32[1,2,64]{2,1,0:T(2,128)} %param.16) | copy-start | bytes 1540

commit v2 on v1

--- a/solution.py
+++ b/solution.py
@@ -14,7 +14,8 @@
 message_scale = 0.0884
 radial_step = 1.25
 block_atoms = 16
-UNROLL = 2
+ROWS = 512
+COLS = 256
 
 
 def iota(shape, dim):
@@ -62,9 +63,11 @@
 
 def kernel(
     F, D, atoms, cap, width,
-    feat, pos, nbr, cnt, send, frames, w_edge, b_edge, w_msg_h, w_upd_h, w_read_h, w_heads,
+    feat_h, pos_h, nbr_h, cnt_h, send_h, frames_h, w_edge_h, b_edge_h, w_msg_h, w_upd_h, w_read_h,
+    w_heads_h,
     out,
-    table, cols, nbr_s, add_s, own_u, send_buf, ghost_buf, lhs, fr_stage, fr_s, base_s, wst,
+    feat, pos, nbr, cnt, send, frames, w_edge, b_edge, w_heads,
+    left_s, wgt_s, table, nbr_s, add_s, own_u, send_buf, ghost_buf, lhs, fr_stage, fr_s, base_s, wst,
     msg_s, z_s, fin_stage, fin_s, w_msg, w_upd, w_read,
     w_sem, halo_send, halo_recv, fr_send, fr_recv, fin_send, fin_recv,
 ):
@@ -85,16 +88,21 @@
         pl.semaphore_signal(barrier, inc=1, device_id={"frame": peer}, device_id_type=MESH)
     for near in (up, down):
         pl.semaphore_signal(barrier, inc=1, device_id={"dom": near}, device_id_type=MESH)
-    weight_copies = [
-        pltpu.make_async_copy(src, dst, w_sem.at[n])
-        for n, (src, dst) in enumerate(((w_msg_h, w_msg), (w_upd_h, w_upd), (w_read_h, w_read)))
-    ]
-    for copy in weight_copies:
+    moves = (
+        (pos_h, pos), (cnt_h, cnt), (send_h, send), (feat_h, feat), (frames_h, frames),
+        (nbr_h, nbr), (w_edge_h, w_edge), (b_edge_h, b_edge),
+        (w_msg_h, w_msg), (w_upd_h, w_upd), (w_read_h, w_read), (w_heads_h, w_heads),
+    )
+    copies = [pltpu.make_async_copy(src, dst, w_sem.at[n]) for n, (src, dst) in enumerate(moves)]
+    for copy in copies:
         copy.start()
+    early, weight_copies = copies[:8], copies[8:]
 
     lane = iota((128, 128), 1)
     row = iota((128, 128), 0)
 
+    for copy in early:
+        copy.wait()
     table[...] = jnp.zeros_like(table)
     table[0:3, :] = pos[...].astype(F32)
     table[3:4, :] = cnt[...].astype(F32)
@@ -225,38 +233,39 @@
     group = lane1 // 8
     special1 = lane1 % 8 >= 6
 
-    def atom(l, i, n, offset, first_id, load_feat, add):
-        local = block_rows(l) + i
-        ids = (first_id + iota((n, 128), 0)).astype(F32)
-        named = nbr_s[pl.ds(first + local, 1), :]
-        mult = jnp.sum(jnp.where(ids == named, 1.0, 0.0), axis=1, keepdims=True)
-        weighted = load_feat() * mult.astype(BF16)
-        mask = jnp.where((group == i) & (~special1), 1.0, 0.0)
-        extra = add_s[pl.ds(first + local, 1), :]
-        left1 = lhs[l * region + offset : l * region + offset + n, 0:128] * mask.astype(BF16)
-        left2 = lhs[l * region + offset : l * region + offset + n, 128:256]
-        left2 = left2 * jnp.where(special1, 1.0, mask).astype(BF16) + extra.astype(BF16)
-        left = jnp.concatenate([left1, left2], axis=1)
-        for fr in range(F):
-            h = dot(left, wst[:, fr * width : (fr + 1) * width]).astype(BF16)
-            terms = (h + h * jnp.tanh(h)) * weighted
-            parts = [terms[k : k + 16, :] for k in range(0, n, 16)]
-            while len(parts) > 1:
-                parts = [sum(parts[k + 1 : k + 2], parts[k]) for k in range(0, len(parts), 2)]
-            total = jnp.sum(parts[0].astype(F32), axis=0, keepdims=True)
-            spot = pl.ds(fr * nat + local, 1)
-            if add:
-                msg_s[spot, :] = msg_s[spot, :] + total
-            else:
-                msg_s[spot, :] = total
-
     def sweep(l, n, offset, first_id, load_feat, add):
+        many = max(k for k in (1, 2, 4, 8, 16) if k * n <= ROWS)
+
         def step(k, _):
-            for j in range(UNROLL):
-                atom(l, k * UNROLL + j, n, offset, first_id, load_feat, add)
+            ids = (first_id + iota((n, 128), 0)).astype(F32)
+            for j in range(many):
+                i = k * many + j
+                own_row = pl.ds(first + block_rows(l) + i, 1)
+                mult = jnp.sum(jnp.where(ids == nbr_s[own_row, :], 1.0, 0.0), axis=1, keepdims=True)
+                wgt_s[j * n : (j + 1) * n, :] = load_feat() * mult.astype(BF16)
+                mask = jnp.where((group == i) & (~special1), 1.0, 0.0)
+                left1 = lhs[l * region + offset : l * region + offset + n, 0:128] * mask.astype(BF16)
+                left2 = lhs[l * region + offset : l * region + offset + n, 128:256]
+                left2 = left2 * jnp.where(special1, 1.0, mask).astype(BF16) + add_s[own_row, :].astype(BF16)
+                left_s[j * n : (j + 1) * n, 0:128] = left1
+                left_s[j * n : (j + 1) * n, 128:256] = left2
+            for c in range(F * width // COLS):
+                fr, lanes = divmod(c * COLS, width)
+                h = dot(left_s[0 : many * n, :], wst[:, c * COLS : (c + 1) * COLS]).astype(BF16)
+                terms = (h + h * jnp.tanh(h)) * wgt_s[0 : many * n, lanes : lanes + COLS]
+                for j in range(many):
+                    parts = [terms[j * n + r : j * n + r + 16, :] for r in range(0, n, 16)]
+                    while len(parts) > 1:
+                        parts = [sum(parts[r + 1 : r + 2], parts[r]) for r in range(0, len(parts), 2)]
+                    total = jnp.sum(parts[0].astype(F32), axis=0, keepdims=True)
+                    spot = pl.ds(fr * nat + block_rows(l) + k * many + j, 1)
+                    if add:
+                        msg_s[spot, lanes : lanes + COLS] = msg_s[spot, lanes : lanes + COLS] + total
+                    else:
+                        msg_s[spot, lanes : lanes + COLS] = total
             return 0
 
-        lax.fori_loop(0, block_atoms // UNROLL, step, 0)
+        lax.fori_loop(0, block_atoms // many, step, 0)
 
     for l in range(per):
         base = own_base(l)
@@ -320,16 +329,26 @@
     slots = neighbours.shape[1]
     per = atoms // block_atoms // F
     vmem = pl.BlockSpec(memory_space=pltpu.VMEM)
-    hbm = pl.BlockSpec(memory_space=pl.ANY)
+    hbm = pl.BlockSpec(memory_space=pltpu.HBM)
     dma = pltpu.SemaphoreType.DMA
     return pl.pallas_call(
         functools.partial(kernel, F, D, atoms, cap, width),
         out_shape=jax.ShapeDtypeStruct((4, atoms), F32),
-        in_specs=[vmem] * 8 + [hbm] * 3 + [vmem],
+        in_specs=[hbm] * 12,
         out_specs=vmem,
         scratch_shapes=[
+            pltpu.VMEM((atoms, width), BF16),
+            pltpu.VMEM((3, atoms), BF16),
+            pltpu.VMEM((atoms, slots), jnp.int32),
+            pltpu.VMEM((1, atoms), jnp.int32),
+            pltpu.VMEM((2, cap), jnp.int32),
+            pltpu.VMEM((3, 1, 3), F32),
+            pltpu.VMEM((w_edge.shape[0], width), F32),
+            pltpu.VMEM((1, width), F32),
+            pltpu.VMEM((4, width), BF16),
+            pltpu.VMEM((ROWS, 256), BF16),
+            pltpu.VMEM((ROWS, width), BF16),
             pltpu.VMEM((128, atoms), F32),
-            pltpu.VMEM((8, 128), F32),
             pltpu.VMEM((atoms, slots), F32),
             pltpu.VMEM((atoms, 128), F32),
             pltpu.VMEM((atoms, 128), BF16),
@@ -347,7 +366,7 @@
             pltpu.VMEM((width, width), BF16),
             pltpu.VMEM((width, width), BF16),
             pltpu.VMEM((width, width), BF16),
-            dma((3,)),
+            dma((12,)),
             dma,
             dma,
             dma((F - 1,)),
@@ -356,7 +375,7 @@
             dma((F - 1,)),
         ],
         compiler_params=pltpu.CompilerParams(
-            collective_id=0, has_side_effects=True, vmem_limit_bytes=48 * 1024 * 1024
+            collective_id=0, has_side_effects=True, vmem_limit_bytes=63 * 1024 * 1024
         ),
     )(
         features, positions, neighbours, counts.reshape(1, -1), send_rows.reshape(2, cap),

time: 41.8 us -> 24.9 us (0.60)
  Pallas kernels: 33.7 us -> 23.4 us
  local copies, waits for them, and re-layouts: 7.62 us -> 1.26 us
    pallas_call x1, Pallas kernels: 33.7 us -> 23.4 us  [local(): pl.pallas_call(functools.partial(kernel, F, D, atoms, cap, width), out_sh...]
    unnamed x25 -> x1, local copies, waits for them, and re-layouts: 7.62 us -> 1.26 us
where the time goes in v2:
time: 24.9 us; the launch traced here: 24.7 us
  Pallas kernels  23.4 us (94%)
  local copies, waits for them, and re-layouts  1.26 us (5%)
    pallas_call x1, Pallas kernels, local(): pl.pallas_call(functools.partial(kernel, F, D, atoms, cap, width), out_sh...  23.4 us
    unnamed x1, local copies, waits for them, and re-layouts  1.26 us

profile of v2, /device:TPU:0, one launch (start us, length us, event | category | flops | bytes accessed | tf_op | source)
XLA Modules:
  0.0 24.7 jit_solution(4370025041367990651)
XLA Ops:
  0.0 23.4 %shard_map.118 = f32[4,128]{1,0:T(4,128)} custom-call(bf16[128,512]{1,0:T(8,128)(2,1)} %feat_h.1, bf16[3,128]{1,0:T(4,128)(2,1)} %pos_h.1, s32[128,128]{1,0:T(8,128)} %nbr_h.1, s32[1,128]{1,0:T(1,128)} %bitcast.9, s32[2,64]{1,0:T(2,128)} %bitcast.8, f32[3,1,3]{2,1,0:T(1,128)} %bitcast.7, f32[9,512]{1,0:T(8,128)} %w_edge_h.1, f32[1,512]{1,0:T(1,128)} %bitcast.6, ...), custom_call_target="tpu_custom_call" | custom-call | tf_op jit(solution)/shard_map/pallas_call | solution.py:334
  23.4 1.3 %copy.14 = f32[4,128]{1,0:T(4,128)} copy(f32[4,128]{1,0:T(4,128)} %shard_map.118) | data formatting | bytes 4096

commit v3 on v2

--- a/solution.py
+++ b/solution.py
@@ -96,13 +96,17 @@
     copies = [pltpu.make_async_copy(src, dst, w_sem.at[n]) for n, (src, dst) in enumerate(moves)]
     for copy in copies:
         copy.start()
-    early, weight_copies = copies[:8], copies[8:]
+    weight_copies = copies[8:]
 
     lane = iota((128, 128), 1)
     row = iota((128, 128), 0)
-
-    for copy in early:
-        copy.wait()
+    lane1 = iota((1, 128), 1)
+    group = lane1 >> 3
+    radial = lane1 & 7
+    special1 = radial >= 6
+
+    copies[0].wait()
+    copies[1].wait()
     table[...] = jnp.zeros_like(table)
     table[0:3, :] = pos[...].astype(F32)
     table[3:4, :] = cnt[...].astype(F32)
@@ -117,45 +121,42 @@
     u = jnp.where((lane >= 6) & (lane < 9), 1.0, u)
     own_u[...] = u.astype(BF16)
 
+    copies[4].wait()
     fr_stage[...] = jnp.zeros_like(fr_stage)
     for a in range(3):
         fr_stage[a : a + 1, 0:3] = frames[a]
-    fr_s[f] = fr_stage[...]
+    fr_s[0] = fr_stage[...]
+    copies[2].wait()
+    copies[3].wait()
     chosen = jnp.where(side == 0, send[1:2, :], send[0:1, :])
     pick = (iota((atoms, cap), 0) == chosen).astype(F32).T.astype(BF16)
     send_buf[:, 0:width] = dot(pick, feat[...]).astype(BF16)
     send_buf[:, width : width + 128] = dot(pick, own_u[...]).astype(BF16)
-
-    pl.semaphore_wait(barrier, F + 1)
-    target = jnp.where(side == 0, up, down)
     halo = pltpu.make_async_remote_copy(
         src_ref=send_buf, dst_ref=ghost_buf, send_sem=halo_send, recv_sem=halo_recv,
-        device_id={"dom": target}, device_id_type=MESH,
+        device_id={"dom": jnp.where(side == 0, up, down)}, device_id_type=MESH,
     )
     fr_copies = [
         pltpu.make_async_remote_copy(
-            src_ref=fr_stage, dst_ref=fr_s.at[f], send_sem=fr_send.at[k], recv_sem=fr_recv.at[k],
-            device_id={"frame": peer}, device_id_type=MESH,
+            src_ref=fr_stage, dst_ref=fr_s.at[F - k], send_sem=fr_send.at[k - 1],
+            recv_sem=fr_recv.at[F - k - 1], device_id={"frame": peers[k - 1]}, device_id_type=MESH,
         )
-        for k, peer in enumerate(peers)
+        for k in range(1, F)
     ]
-    for copy in fr_copies:
-        copy.start()
-    halo.start()
-
+
+    copies[5].wait()
     live = iota((atoms, nbr.shape[1]), 1).astype(F32) < by_atom[:, 3:4]
     nbr_s[...] = jnp.where(live, nbr[...].astype(F32), -1.0)
 
-    radial = lane % 8
-    spot = (lane // 8) * 2 + radial - 6
-    special = radial >= 6
-    place = special & (spot < 6) & (row < 3) & (row == spot % 3)
-    place_neg = special & (spot >= 6) & (spot < 12) & (row < 3) & (row == spot % 3)
-    place_one = special & (spot >= 12) & (spot < 14) & (row == 6)
-    place_add = jnp.where(place_one, 1.0, jnp.where(place_neg, -1.0, 0.0)).astype(BF16)
+    spot = jnp.where(special1, group * 2 + radial - 6, -1)
+    place_row = jnp.where(spot < 3, spot, jnp.where(spot < 6, spot - 3, -1))
+    neg_row = jnp.where((spot >= 6) & (spot < 9), spot - 6, -1)
+    neg_row = jnp.where((spot >= 9) & (spot < 12), spot - 9, neg_row)
+    one_row = jnp.where((spot >= 12) & (spot < 14), 6, -1)
+    place_add = jnp.where(row == one_row, 1.0, jnp.where(row == neg_row, -1.0, 0.0)).astype(BF16)
     add_s[...] = dot(own_u[...], place_add)
-    place = jnp.where(place, 1.0, 0.0).astype(BF16)
-    centres = radial[0:1, :].astype(F32) * radial_step
+    place = jnp.where(row == place_row, 1.0, 0.0).astype(BF16)
+    centres = radial.astype(F32) * radial_step
 
     def block_rows(l):
         return (l * (1 - side) + (per - 1 - l) * side) * block_atoms
@@ -168,29 +169,28 @@
 
     def geometry(l):
         start = first + block_rows(l)
-        expand = jnp.where(row == start + lane // 8, 1.0, 0.0).astype(BF16)
+        expand = jnp.where(row == start + group, 1.0, 0.0).astype(BF16)
         centre = dot(table[0:16, :].astype(BF16), expand)
         sub = iota((16, 128), 0)
         sqi = jnp.sum(jnp.where(sub < 3, centre * centre, 0.0), axis=0, keepdims=True) + 0.25
         hi, tail = split(sqi)
         mid, lo = split(tail)
-        g = jnp.where((row >= 3) & (row < 6), 1.0, 0.0)
-        for c in range(3):
-            g = jnp.where(row == c, -2.0 * centre[c : c + 1, :], g)
+        g = jnp.where(sub < 3, -2.0 * centre, jnp.where(sub < 6, 1.0, 0.0))
         for c, part in enumerate((hi, mid, lo)):
-            g = jnp.where(row == 6 + c, part, g)
-        return g.astype(BF16)
+            g = jnp.where(sub == 6 + c, part, g)
+        g = jnp.concatenate([g.astype(BF16), jnp.zeros((112, 128), BF16)], axis=0)
+        return jnp.concatenate([g, place], axis=1)
 
     def fill(l, g, rows_u, offset):
         n = rows_u.shape[0]
-        d2 = dot(rows_u, g)
-        placed = dot(rows_u, place)
+        both = dot(rows_u, g)
+        d2, placed = both[:, 0:128], both[:, 128:256]
         dist = jnp.sqrt(jnp.maximum(d2, 0.25))
         gap = dist - centres
         value = jnp.exp(-(gap * gap))
-        spec = special[0:n, :]
-        lhs[l * region + offset : l * region + offset + n, 0:128] = jnp.where(spec, 0.0, value).astype(BF16)
-        lhs[l * region + offset : l * region + offset + n, 128:256] = jnp.where(spec, placed, value).astype(BF16)
+        at = l * region + offset
+        lhs[at : at + n, 0:128] = jnp.where(special1, 0.0, value).astype(BF16)
+        lhs[at : at + n, 128:256] = jnp.where(special1, placed, value).astype(BF16)
 
     gs = []
     for l in range(per):
@@ -198,18 +198,16 @@
         gs.append(g)
         fill(l, g, own_u[pl.ds(own_base(l), own_n[l]), :], 0)
 
-    r = iota((256, 32), 0)
-    c = iota((256, 32), 1)
-    rb = r % 8
-    rs = (r % 128) // 8 * 2 + rb - 6
-    second = r // 128
-    want = jnp.where(rb < 6, second * 6 + rb, -1)
-    sp = (rb >= 6) & (second == 1)
-    want = jnp.where(sp & (rs < 3), 12 + rs, want)
-    want = jnp.where(sp & (rs >= 3) & (rs < 6), 12 + rs, want)
-    want = jnp.where(sp & (rs >= 6) & (rs < 12), 6 + rs, want)
-    want = jnp.where(sp & (rs >= 12) & (rs < 14), 6 + rs, want)
-    sel = jnp.where(want == c, 1.0, 0.0).astype(BF16)
+    def wanted(second):
+        want = jnp.where(special1, -1, radial + 6 * second)
+        if second:
+            want = jnp.where((spot >= 0) & (spot < 6), spot + 12, want)
+            want = jnp.where((spot >= 6) & (spot < 14), spot + 6, want)
+        return jnp.where(iota((32, 128), 0) == want, 1.0, 0.0).T.astype(BF16)
+
+    sel = jnp.concatenate([wanted(0), wanted(1)], axis=0)
+    copies[6].wait()
+    copies[7].wait()
     base_s[...] = jnp.zeros_like(base_s)
     hi, lo = split(0.5 * w_edge[0:6, :])
     base_s[0:6, :] = hi
@@ -217,9 +215,8 @@
     hi, lo = split(0.5 * b_edge[...])
     base_s[18:19, :] = hi
     base_s[19:20, :] = lo
-    for copy in fr_copies:
-        copy.wait()
-    for fr in range(F):
+
+    def edge_weights(fr):
         for cc in range(3):
             acc = fr_s[fr, 0:1, cc : cc + 1] * w_edge[6:7, :]
             acc = acc + fr_s[fr, 1:2, cc : cc + 1] * w_edge[7:8, :]
@@ -229,47 +226,67 @@
             base_s[15 + cc : 16 + cc, :] = lo
         wst[:, fr * width : (fr + 1) * width] = dot(sel, base_s[...].astype(BF16)).astype(BF16)
 
-    lane1 = iota((1, 128), 1)
-    group = lane1 // 8
-    special1 = lane1 % 8 >= 6
-
-    def sweep(l, n, offset, first_id, load_feat, add):
+    edge_weights(0)
+
+    own_at = [block_atoms * sum(own_n[:l]) for l in range(per)]
+    ghost_at = [block_atoms * (sum(own_n) + sum(ghost_n[:l])) for l in range(per)]
+
+    def sweep(l, n, at, offset, first_id, load_feat, build, slots, add):
         many = max(k for k in (1, 2, 4, 8, 16) if k * n <= ROWS)
 
         def step(k, _):
             ids = (first_id + iota((n, 128), 0)).astype(F32)
-            for j in range(many):
+            here = pl.multiple_of(at + k * (many * n), 16)
+            for j in range(many if build else 0):
                 i = k * many + j
+                rows = pl.ds(pl.multiple_of(here + j * n, 16), n)
                 own_row = pl.ds(first + block_rows(l) + i, 1)
                 mult = jnp.sum(jnp.where(ids == nbr_s[own_row, :], 1.0, 0.0), axis=1, keepdims=True)
-                wgt_s[j * n : (j + 1) * n, :] = load_feat() * mult.astype(BF16)
+                wgt_s[rows, :] = load_feat() * mult.astype(BF16)
                 mask = jnp.where((group == i) & (~special1), 1.0, 0.0)
                 left1 = lhs[l * region + offset : l * region + offset + n, 0:128] * mask.astype(BF16)
                 left2 = lhs[l * region + offset : l * region + offset + n, 128:256]
                 left2 = left2 * jnp.where(special1, 1.0, mask).astype(BF16) + add_s[own_row, :].astype(BF16)
-                left_s[j * n : (j + 1) * n, 0:128] = left1
-                left_s[j * n : (j + 1) * n, 128:256] = left2
-            for c in range(F * width // COLS):
-                fr, lanes = divmod(c * COLS, width)
-                h = dot(left_s[0 : many * n, :], wst[:, c * COLS : (c + 1) * COLS]).astype(BF16)
-                terms = (h + h * jnp.tanh(h)) * wgt_s[0 : many * n, lanes : lanes + COLS]
-                for j in range(many):
-                    parts = [terms[j * n + r : j * n + r + 16, :] for r in range(0, n, 16)]
-                    while len(parts) > 1:
-                        parts = [sum(parts[r + 1 : r + 2], parts[r]) for r in range(0, len(parts), 2)]
-                    total = jnp.sum(parts[0].astype(F32), axis=0, keepdims=True)
-                    spot = pl.ds(fr * nat + block_rows(l) + k * many + j, 1)
-                    if add:
-                        msg_s[spot, lanes : lanes + COLS] = msg_s[spot, lanes : lanes + COLS] + total
-                    else:
+                left_s[rows, 0:128] = left1
+                left_s[rows, 128:256] = left2
+            for fr in slots:
+                for lanes in range(0, width, COLS):
+                    c = fr * width + lanes
+                    h = dot(left_s[pl.ds(here, many * n), :], wst[:, c : c + COLS]).astype(BF16)
+                    terms = (h + h * jnp.tanh(h)) * wgt_s[pl.ds(here, many * n), lanes : lanes + COLS]
+                    for j in range(many):
+                        parts = [terms[j * n + r : j * n + r + 16, :] for r in range(0, n, 16)]
+                        while len(parts) > 1:
+                            parts = [sum(parts[r + 1 : r + 2], parts[r]) for r in range(0, len(parts), 2)]
+                        total = jnp.sum(parts[0].astype(F32), axis=0, keepdims=True)
+                        spot = pl.ds(fr * nat + block_rows(l) + k * many + j, 1)
+                        if add:
+                            total = total + msg_s[spot, lanes : lanes + COLS]
                         msg_s[spot, lanes : lanes + COLS] = total
             return 0
 
         lax.fori_loop(0, block_atoms // many, step, 0)
 
-    for l in range(per):
+    def own_sweep(l, build, slots):
         base = own_base(l)
-        sweep(l, own_n[l], 0, base, lambda l=l, base=base: feat[pl.ds(base, own_n[l]), :], False)
+        sweep(
+            l, own_n[l], own_at[l], 0, base, lambda: feat[pl.ds(base, own_n[l]), :], build, slots, False
+        )
+
+    order = list(range(per))
+    for l in order[:-1]:
+        own_sweep(l, True, [0])
+    pl.semaphore_wait(barrier, F + 1)
+    for copy in fr_copies:
+        copy.start()
+    halo.start()
+    own_sweep(order[-1], True, [0])
+    for copy in fr_copies:
+        copy.wait()
+    for k in range(1, F):
+        edge_weights(k)
+    for l in order:
+        own_sweep(l, False, list(range(1, F)))
 
     halo.wait()
     for l in range(per):
@@ -278,8 +295,9 @@
         base = ghost_base(l)
         fill(l, gs[l], ghost_buf[pl.ds(base, ghost_n[l]), width : width + 128], atoms)
         sweep(
-            l, ghost_n[l], atoms, atoms + side * cap + base,
+            l, ghost_n[l], ghost_at[l], atoms, atoms + side * cap + base,
             lambda l=l, base=base: ghost_buf[pl.ds(base, ghost_n[l]), 0:width], True,
+            list(range(F)), True,
         )
 
     for copy in weight_copies:
@@ -328,6 +346,7 @@
     cap = send_rows.shape[2]
     slots = neighbours.shape[1]
     per = atoms // block_atoms // F
+    rows = block_atoms * sum(sum(sizes) for sizes in chunk_sizes(F, atoms, cap))
     vmem = pl.BlockSpec(memory_space=pltpu.VMEM)
     hbm = pl.BlockSpec(memory_space=pltpu.HBM)
     dma = pltpu.SemaphoreType.DMA
@@ -346,8 +365,8 @@
             pltpu.VMEM((w_edge.shape[0], width), F32),
             pltpu.VMEM((1, width), F32),
             pltpu.VMEM((4, width), BF16),
-            pltpu.VMEM((ROWS, 256), BF16),
-            pltpu.VMEM((ROWS, width), BF16),
+            pltpu.VMEM((rows, 256), BF16),
+            pltpu.VMEM((rows, width), BF16),
             pltpu.VMEM((128, atoms), F32),
             pltpu.VMEM((atoms, slots), F32),
             pltpu.VMEM((atoms, 128), F32),

time: 24.9 us -> 23.9 us (0.960)
  Pallas kernels: 23.4 us -> 22.5 us
    pallas_call x1, Pallas kernels: 23.4 us -> 22.5 us  [local(): pl.pallas_call(functools.partial(kernel, F, D, atoms, cap, width), out_sh...]
where the time goes in v3:
time: 23.9 us; the launch traced here: 23.7 us
  Pallas kernels  22.5 us (94%)
  local copies, waits for them, and re-layouts  1.26 us (5%)
    pallas_call x1, Pallas kernels, local(): pl.pallas_call(functools.partial(kernel, F, D, atoms, cap, width), out_sh...  22.5 us
    unnamed x1, local copies, waits for them, and re-layouts  1.26 us

profile of v3, /device:TPU:0, one launch (start us, length us, event | category | flops | bytes accessed | tf_op | source)
XLA Modules:
  0.0 23.7 jit_solution(208358707660897857)
XLA Ops:
  0.0 22.5 %shard_map.118 = f32[4,128]{1,0:T(4,128)} custom-call(bf16[128,512]{1,0:T(8,128)(2,1)} %feat_h.1, bf16[3,128]{1,0:T(4,128)(2,1)} %pos_h.1, s32[128,128]{1,0:T(8,128)} %nbr_h.1, s32[1,128]{1,0:T(1,128)} %bitcast.9, s32[2,64]{1,0:T(2,128)} %bitcast.8, f32[3,1,3]{2,1,0:T(1,128)} %bitcast.7, f32[9,512]{1,0:T(8,128)} %w_edge_h.1, f32[1,512]{1,0:T(1,128)} %bitcast.6, ...), custom_call_target="tpu_custom_call" | custom-call | tf_op jit(solution)/shard_map/pallas_call | solution.py:353
  22.5 1.3 %copy.14 = f32[4,128]{1,0:T(4,128)} copy(f32[4,128]{1,0:T(4,128)} %shard_map.118) | data formatting | bytes 4096

commit v4 on v3

--- a/solution.py
+++ b/solution.py
@@ -14,7 +14,7 @@
 message_scale = 0.0884
 radial_step = 1.25
 block_atoms = 16
-ROWS = 512
+ROWS = 2048
 COLS = 256
 
 
@@ -265,7 +265,10 @@
                         msg_s[spot, lanes : lanes + COLS] = total
             return 0
 
-        lax.fori_loop(0, block_atoms // many, step, 0)
+        if many == block_atoms:
+            step(0, 0)
+        else:
+            lax.fori_loop(0, block_atoms // many, step, 0)
 
     def own_sweep(l, build, slots):
         base = own_base(l)
@@ -273,20 +276,22 @@
             l, own_n[l], own_at[l], 0, base, lambda: feat[pl.ds(base, own_n[l]), :], build, slots, False
         )
 
-    order = list(range(per))
-    for l in order[:-1]:
-        own_sweep(l, True, [0])
+    order = list(range(per))[::-1]
+    own_sweep(order[0], True, [0])
     pl.semaphore_wait(barrier, F + 1)
     for copy in fr_copies:
         copy.start()
     halo.start()
-    own_sweep(order[-1], True, [0])
+    for l in order[1:2]:
+        own_sweep(l, True, [0])
     for copy in fr_copies:
         copy.wait()
     for k in range(1, F):
         edge_weights(k)
-    for l in order:
+    for l in order[:2]:
         own_sweep(l, False, list(range(1, F)))
+    for l in order[2:]:
+        own_sweep(l, True, list(range(F)))
 
     halo.wait()
     for l in range(per):

time: 23.9 us -> 20.8 us (0.87)
  Pallas kernels: 22.5 us -> 19.4 us
    pallas_call x1, Pallas kernels: 22.5 us -> 19.4 us  [local(): pl.pallas_call(functools.partial(kernel, F, D, atoms, cap, width), out_sh...]
where the time goes in v4:
time: 20.8 us; the launch traced here: 20.6 us
  Pallas kernels  19.4 us (93%)
  local copies, waits for them, and re-layouts  1.26 us (6%)
    pallas_call x1, Pallas kernels, local(): pl.pallas_call(functools.partial(kernel, F, D, atoms, cap, width), out_sh...  19.4 us
    unnamed x1, local copies, waits for them, and re-layouts  1.26 us

profile of v4, /device:TPU:0, one launch (start us, length us, event | category | flops | bytes accessed | tf_op | source)
XLA Modules:
  0.0 20.6 jit_solution(14263408536238454312)
XLA Ops:
  0.0 19.4 %shard_map.118 = f32[4,128]{1,0:T(4,128)} custom-call(bf16[128,512]{1,0:T(8,128)(2,1)} %feat_h.1, bf16[3,128]{1,0:T(4,128)(2,1)} %pos_h.1, s32[128,128]{1,0:T(8,128)} %nbr_h.1, s32[1,128]{1,0:T(1,128)} %bitcast.9, s32[2,64]{1,0:T(2,128)} %bitcast.8, f32[3,1,3]{2,1,0:T(1,128)} %bitcast.7, f32[9,512]{1,0:T(8,128)} %w_edge_h.1, f32[1,512]{1,0:T(1,128)} %bitcast.6, ...), custom_call_target="tpu_custom_call" | custom-call | tf_op jit(solution)/shard_map/pallas_call | solution.py:358
  19.4 1.3 %copy.14 = f32[4,128]{1,0:T(4,128)} copy(f32[4,128]{1,0:T(4,128)} %shard_map.118) | data formatting | bytes 4096

commit v5 on v3

--- a/solution.py
+++ b/solution.py
@@ -68,7 +68,7 @@
     out,
     feat, pos, nbr, cnt, send, frames, w_edge, b_edge, w_heads,
     left_s, wgt_s, table, nbr_s, add_s, own_u, send_buf, ghost_buf, lhs, fr_stage, fr_s, base_s, wst,
-    msg_s, z_s, fin_stage, fin_s, w_msg, w_upd, w_read,
+    msg_s, acc_s, z_s, fin_stage, fin_s, w_msg, w_upd, w_read,
     w_sem, halo_send, halo_recv, fr_send, fr_recv, fin_send, fin_recv,
 ):
     f = lax.axis_index("frame")
@@ -231,15 +231,35 @@
     own_at = [block_atoms * sum(own_n[:l]) for l in range(per)]
     ghost_at = [block_atoms * (sum(own_n) + sum(ghost_n[:l])) for l in range(per)]
 
-    def sweep(l, n, at, offset, first_id, load_feat, build, slots, add):
+    pending = []
+
+    def flush():
+        while pending:
+            pending.pop()()
+
+    def finish(h, at, n, atoms_here, fr, lanes, last):
+        terms = (h + h * jnp.tanh(h)) * wgt_s[at : at + len(atoms_here) * n, lanes : lanes + COLS]
+        for j, local in enumerate(atoms_here):
+            parts = [terms[j * n + r : j * n + r + 16, :] for r in range(0, n, 16)]
+            while len(parts) > 1:
+                parts = [sum(parts[r + 1 : r + 2], parts[r]) for r in range(0, len(parts), 2)]
+            total = parts[0].astype(F32)
+            total = total[0:8, :] + total[8:16, :]
+            eight = pl.ds(pl.multiple_of((fr * nat + local) * 8, 8), 8)
+            if last:
+                total = total + acc_s[eight, lanes : lanes + COLS]
+                spot = pl.ds(fr * nat + local, 1)
+                msg_s[spot, lanes : lanes + COLS] = jnp.sum(total, axis=0, keepdims=True)
+            else:
+                acc_s[eight, lanes : lanes + COLS] = total
+
+    def sweep(l, n, at, offset, first_id, load_feat, build, slots, last):
         many = max(k for k in (1, 2, 4, 8, 16) if k * n <= ROWS)
-
-        def step(k, _):
-            ids = (first_id + iota((n, 128), 0)).astype(F32)
-            here = pl.multiple_of(at + k * (many * n), 16)
-            for j in range(many if build else 0):
-                i = k * many + j
-                rows = pl.ds(pl.multiple_of(here + j * n, 16), n)
+        ids = (first_id + iota((n, 128), 0)).astype(F32)
+        for k in range(0, block_atoms, many):
+            here = at + k * n
+            for i in range(k, k + many if build else k):
+                rows = slice(at + i * n, at + i * n + n)
                 own_row = pl.ds(first + block_rows(l) + i, 1)
                 mult = jnp.sum(jnp.where(ids == nbr_s[own_row, :], 1.0, 0.0), axis=1, keepdims=True)
                 wgt_s[rows, :] = load_feat() * mult.astype(BF16)
@@ -249,23 +269,13 @@
                 left2 = left2 * jnp.where(special1, 1.0, mask).astype(BF16) + add_s[own_row, :].astype(BF16)
                 left_s[rows, 0:128] = left1
                 left_s[rows, 128:256] = left2
+            atoms_here = [block_rows(l) + i for i in range(k, k + many)]
             for fr in slots:
                 for lanes in range(0, width, COLS):
                     c = fr * width + lanes
-                    h = dot(left_s[pl.ds(here, many * n), :], wst[:, c : c + COLS]).astype(BF16)
-                    terms = (h + h * jnp.tanh(h)) * wgt_s[pl.ds(here, many * n), lanes : lanes + COLS]
-                    for j in range(many):
-                        parts = [terms[j * n + r : j * n + r + 16, :] for r in range(0, n, 16)]
-                        while len(parts) > 1:
-                            parts = [sum(parts[r + 1 : r + 2], parts[r]) for r in range(0, len(parts), 2)]
-                        total = jnp.sum(parts[0].astype(F32), axis=0, keepdims=True)
-                        spot = pl.ds(fr * nat + block_rows(l) + k * many + j, 1)
-                        if add:
-                            total = total + msg_s[spot, lanes : lanes + COLS]
-                        msg_s[spot, lanes : lanes + COLS] = total
-            return 0
-
-        lax.fori_loop(0, block_atoms // many, step, 0)
+                    h = dot(left_s[here : here + many * n, :], wst[:, c : c + COLS]).astype(BF16)
+                    flush()
+                    pending.append(functools.partial(finish, h, here, n, atoms_here, fr, lanes, last))
 
     def own_sweep(l, build, slots):
         base = own_base(l)
@@ -273,25 +283,28 @@
             l, own_n[l], own_at[l], 0, base, lambda: feat[pl.ds(base, own_n[l]), :], build, slots, False
         )
 
-    order = list(range(per))
-    for l in order[:-1]:
+    order = list(range(per))[::-1]
+    for l in order[:2]:
         own_sweep(l, True, [0])
     pl.semaphore_wait(barrier, F + 1)
     for copy in fr_copies:
         copy.start()
     halo.start()
-    own_sweep(order[-1], True, [0])
+    for l in order[2:3]:
+        own_sweep(l, True, [0])
     for copy in fr_copies:
         copy.wait()
     for k in range(1, F):
         edge_weights(k)
-    for l in order:
+    for l in order[:3]:
         own_sweep(l, False, list(range(1, F)))
+    for l in order[3:]:
+        own_sweep(l, True, list(range(F)))
 
     halo.wait()
     for l in range(per):
         if ghost_n[l] == 0:
-            continue
+            raise ValueError(l)
         base = ghost_base(l)
         fill(l, gs[l], ghost_buf[pl.ds(base, ghost_n[l]), width : width + 128], atoms)
         sweep(
@@ -299,6 +312,7 @@
             lambda l=l, base=base: ghost_buf[pl.ds(base, ghost_n[l]), 0:width], True,
             list(range(F)), True,
         )
+    flush()
 
     for copy in weight_copies:
         copy.wait()
@@ -379,6 +393,7 @@
             pltpu.VMEM((32, width), F32),
             pltpu.VMEM((256, F * width), BF16),
             pltpu.VMEM((F * per * block_atoms, width), F32),
+            pltpu.VMEM((F * per * block_atoms * 8, width), F32),
             pltpu.VMEM((8, 128), F32),
             pltpu.VMEM((8, 128), F32),
             pltpu.VMEM((F, 8, 128), F32),

time: 23.9 us -> 19.7 us (0.82)
  Pallas kernels: 22.5 us -> 18.2 us
    pallas_call x1, Pallas kernels: 22.5 us -> 18.2 us  [local(): pl.pallas_call(functools.partial(kernel, F, D, atoms, cap, width), out_sh...]
where the time goes in v5:
time: 19.7 us; the launch traced here: 19.5 us
  Pallas kernels  18.2 us (92%)
  local copies, waits for them, and re-layouts  1.26 us (6%)
    pallas_call x1, Pallas kernels, local(): pl.pallas_call(functools.partial(kernel, F, D, atoms, cap, width), out_sh...  18.2 us
    unnamed x1, local copies, waits for them, and re-layouts  1.26 us

profile of v5, /device:TPU:0, one launch (start us, length us, event | category | flops | bytes accessed | tf_op | source)
XLA Modules:
  0.0 19.5 jit_solution(5100376861859090117)
XLA Ops:
  0.0 18.2 %shard_map.118 = f32[4,128]{1,0:T(4,128)} custom-call(bf16[128,512]{1,0:T(8,128)(2,1)} %feat_h.1, bf16[3,128]{1,0:T(4,128)(2,1)} %pos_h.1, s32[128,128]{1,0:T(8,128)} %nbr_h.1, s32[1,128]{1,0:T(1,128)} %bitcast.9, s32[2,64]{1,0:T(2,128)} %bitcast.8, f32[3,1,3]{2,1,0:T(1,128)} %bitcast.7, f32[9,512]{1,0:T(8,128)} %w_edge_h.1, f32[1,512]{1,0:T(1,128)} %bitcast.6, ...), custom_call_target="tpu_custom_call" | custom-call | tf_op jit(solution)/shard_map/pallas_call | solution.py:367
  18.3 1.3 %copy.14 = f32[4,128]{1,0:T(4,128)} copy(f32[4,128]{1,0:T(4,128)} %shard_map.118) | data formatting | bytes 4096

commit v6 on v5

--- a/solution.py
+++ b/solution.py
@@ -15,7 +15,7 @@
 radial_step = 1.25
 block_atoms = 16
 ROWS = 512
-COLS = 256
+COLS = 512
 
 
 def iota(shape, dim):

time: 19.7 us -> 19.7 us (level)
  no operation moved by 1% of the time
where the time goes in v6:
time: 19.7 us; the launch traced here: 19.6 us
  Pallas kernels  18.3 us (93%)
  local copies, waits for them, and re-layouts  1.26 us (6%)
    pallas_call x1, Pallas kernels, local(): pl.pallas_call(functools.partial(kernel, F, D, atoms, cap, width), out_sh...  18.3 us
    unnamed x1, local copies, waits for them, and re-layouts  1.26 us

profile of v6, /device:TPU:0, one launch (start us, length us, event | category | flops | bytes accessed | tf_op | source)
XLA Modules:
  0.0 19.6 jit_solution(18190826916578345767)
XLA Ops:
  0.0 18.3 %shard_map.118 = f32[4,128]{1,0:T(4,128)} custom-call(bf16[128,512]{1,0:T(8,128)(2,1)} %feat_h.1, bf16[3,128]{1,0:T(4,128)(2,1)} %pos_h.1, s32[128,128]{1,0:T(8,128)} %nbr_h.1, s32[1,128]{1,0:T(1,128)} %bitcast.9, s32[2,64]{1,0:T(2,128)} %bitcast.8, f32[3,1,3]{2,1,0:T(1,128)} %bitcast.7, f32[9,512]{1,0:T(8,128)} %w_edge_h.1, f32[1,512]{1,0:T(1,128)} %bitcast.6, ...), custom_call_target="tpu_custom_call" | custom-call | tf_op jit(solution)/shard_map/pallas_call | solution.py:367
  18.3 1.3 %copy.14 = f32[4,128]{1,0:T(4,128)} copy(f32[4,128]{1,0:T(4,128)} %shard_map.118) | data formatting | bytes 4096

commit v7 on v6

--- a/solution.py
+++ b/solution.py
@@ -16,6 +16,7 @@
 block_atoms = 16
 ROWS = 512
 COLS = 512
+HALF = 8
 
 
 def iota(shape, dim):
@@ -238,7 +239,7 @@
             pending.pop()()
 
     def finish(h, at, n, atoms_here, fr, lanes, last):
-        terms = (h + h * jnp.tanh(h)) * wgt_s[at : at + len(atoms_here) * n, lanes : lanes + COLS]
+        terms = (h + h * jnp.tanh(h)) * wgt_s[pl.ds(at, len(atoms_here) * n), lanes : lanes + COLS]
         for j, local in enumerate(atoms_here):
             parts = [terms[j * n + r : j * n + r + 16, :] for r in range(0, n, 16)]
             while len(parts) > 1:
@@ -256,26 +257,35 @@
     def sweep(l, n, at, offset, first_id, load_feat, build, slots, last):
         many = max(k for k in (1, 2, 4, 8, 16) if k * n <= ROWS)
         ids = (first_id + iota((n, 128), 0)).astype(F32)
-        for k in range(0, block_atoms, many):
-            here = at + k * n
-            for i in range(k, k + many if build else k):
-                rows = slice(at + i * n, at + i * n + n)
-                own_row = pl.ds(first + block_rows(l) + i, 1)
-                mult = jnp.sum(jnp.where(ids == nbr_s[own_row, :], 1.0, 0.0), axis=1, keepdims=True)
-                wgt_s[rows, :] = load_feat() * mult.astype(BF16)
-                mask = jnp.where((group == i) & (~special1), 1.0, 0.0)
-                left1 = lhs[l * region + offset : l * region + offset + n, 0:128] * mask.astype(BF16)
-                left2 = lhs[l * region + offset : l * region + offset + n, 128:256]
-                left2 = left2 * jnp.where(special1, 1.0, mask).astype(BF16) + add_s[own_row, :].astype(BF16)
-                left_s[rows, 0:128] = left1
-                left_s[rows, 128:256] = left2
-            atoms_here = [block_rows(l) + i for i in range(k, k + many)]
-            for fr in slots:
-                for lanes in range(0, width, COLS):
-                    c = fr * width + lanes
-                    h = dot(left_s[here : here + many * n, :], wst[:, c : c + COLS]).astype(BF16)
-                    flush()
-                    pending.append(functools.partial(finish, h, here, n, atoms_here, fr, lanes, last))
+        many = min(many, HALF)
+
+        def step(half, _):
+            for k in range(0, HALF, many):
+                here = pl.multiple_of(at + (half * HALF + k) * n, 16)
+                for j in range(many if build else 0):
+                    i = half * HALF + k + j
+                    rows = pl.ds(pl.multiple_of(here + j * n, 16), n)
+                    own_row = pl.ds(first + block_rows(l) + i, 1)
+                    mult = jnp.sum(jnp.where(ids == nbr_s[own_row, :], 1.0, 0.0), axis=1, keepdims=True)
+                    wgt_s[rows, :] = load_feat() * mult.astype(BF16)
+                    mask = jnp.where((group == i) & (~special1), 1.0, 0.0)
+                    left1 = lhs[l * region + offset : l * region + offset + n, 0:128] * mask.astype(BF16)
+                    left2 = lhs[l * region + offset : l * region + offset + n, 128:256]
+                    left2 = left2 * jnp.where(special1, 1.0, mask).astype(BF16) + add_s[own_row, :].astype(BF16)
+                    left_s[rows, 0:128] = left1
+                    left_s[rows, 128:256] = left2
+                atoms_here = [block_rows(l) + half * HALF + k + j for j in range(many)]
+                for fr in slots:
+                    for lanes in range(0, width, COLS):
+                        c = fr * width + lanes
+                        h = dot(left_s[pl.ds(here, many * n), :], wst[:, c : c + COLS]).astype(BF16)
+                        flush()
+                        pending.append(functools.partial(finish, h, here, n, atoms_here, fr, lanes, last))
+            flush()
+            return 0
+
+        flush()
+        lax.fori_loop(0, block_atoms // HALF, step, 0)
 
     def own_sweep(l, build, slots):
         base = own_base(l)

time: 19.7 us -> 22.1 us (1.12)
  Pallas kernels: 18.3 us -> 20.6 us
    pallas_call x1, Pallas kernels: 18.3 us -> 20.6 us  [local(): pl.pallas_call(functools.partial(kernel, F, D, atoms, cap, width), out_sh...]
where the time goes in v7:
time: 22.1 us; the launch traced here: 21.9 us
  Pallas kernels  20.6 us (93%)
  local copies, waits for them, and re-layouts  1.26 us (6%)
    pallas_call x1, Pallas kernels, local(): pl.pallas_call(functools.partial(kernel, F, D, atoms, cap, width), out_sh...  20.6 us
    unnamed x1, local copies, waits for them, and re-layouts  1.26 us

profile of v7, /device:TPU:0, one launch (start us, length us, event | category | flops | bytes accessed | tf_op | source)
XLA Modules:
  0.0 21.9 jit_solution(18154294590677782156)
XLA Ops:
  0.0 20.6 %shard_map.118 = f32[4,128]{1,0:T(4,128)} custom-call(bf16[128,512]{1,0:T(8,128)(2,1)} %feat_h.1, bf16[3,128]{1,0:T(4,128)(2,1)} %pos_h.1, s32[128,128]{1,0:T(8,128)} %nbr_h.1, s32[1,128]{1,0:T(1,128)} %bitcast.9, s32[2,64]{1,0:T(2,128)} %bitcast.8, f32[3,1,3]{2,1,0:T(1,128)} %bitcast.7, f32[9,512]{1,0:T(8,128)} %w_edge_h.1, f32[1,512]{1,0:T(1,128)} %bitcast.6, ...), custom_call_target="tpu_custom_call" | custom-call | tf_op jit(solution)/shard_map/pallas_call | solution.py:377
  20.6 1.3 %copy.14 = f32[4,128]{1,0:T(4,128)} copy(f32[4,128]{1,0:T(4,128)} %shard_map.118) | data formatting | bytes 4096
